TPU v7x, 512 devices: a whole 4x8x8 slice. The times are simulated.
512 devices in a mesh: seq: 256 (over z, x, y_hi, core), head: 2 (over y_lo).
Axes of the slice: x: 4, y: 8 (y_hi: 4, y_lo: 2; y = y_hi * 2 + y_lo), z: 8, core: 2. Of those that a mesh axis runs over, the one named last changes fastest.
Arguments:
- queries: bfloat16 [65536, 2048], P('seq', 'head'), may hold values from -5 to 5
- key_rows: bfloat16 [65536, 2048], P('seq', 'head'), may hold values from -5 to 5
- value_rows: bfloat16 [65536, 2048], P('seq', 'head'), may hold values from -6 to 6
- out_grad: bfloat16 [65536, 2048], P('seq', 'head'), may hold values from -6 to 6
- padding: int32 [65536], P('seq'), may hold values 0 or 1
- header_keys: bfloat16 [256, 2048], P('seq', 'head'), may hold values from -6 to 6
- header_values: bfloat16 [256, 2048], P('seq', 'head'), may hold values from -6 to 6
- neighbours: int32 [512, 5], P('seq'), may hold values from 0 to 511, as said below
- slot_valid: int32 [512, 5], P('seq'), may hold values from 0 to 1, as said below
- crystal_ids: int32 [512], P('seq'), may hold values from 0 to 127, as said below
- header_index: int32 [128, 2], replicated, may hold values from 0 to 255, as said below
Outputs:
- query_grad: bfloat16 [65536, 2048], P(('seq', 'head'))
- key_grad: bfloat16 [65536, 2048], P(('seq', 'head'))
- value_grad: bfloat16 [65536, 2048], P(('seq', 'head'))
- header_key_grad: bfloat16 [256, 2048], P('seq', 'head')
- header_value_grad: bfloat16 [256, 2048], P('seq', 'head')
Inputs may be any that keep to these rules, and one draw needn't show every extreme that they name: `crystal_ids`: crystals are runs of 3 to 5 consecutive token blocks, numbered in order from 0 at block 0; some crystal holds 5 blocks. `neighbours`: slot s of block b names the block of b's crystal at periodic offset 0, +1, -1, +2, -2 (s = 0 to 4) from b, counted modulo the crystal's number of blocks. `slot_valid`: 1 exactly on the first m slots of a block whose crystal holds m blocks. `header_index`: every header row is named by exactly one crystal.
All inputs are finite; a program needn't handle non-finite values. No bound on the sum of `padding` on one device may be relied on, other than what follows from the above.
Results may differ from a plain program's by a relative error of at most 0.0098.
Values may be sent and summed in bfloat16 or wider, within the bound.
A program may use at most 64 MiB of HBM per device.

v0:
```python
import math

import jax
import jax.numpy as jnp
from jax import lax
from jax.sharding import PartitionSpec as P

DH = 128
BLK = 128
REACH = 2


NEG_SCORE = -1e30


def passed_along(block, axis, distance):
    devices = range(lax.axis_size(axis))
    route = [((i - distance) % len(devices), i) for i in devices]
    return lax.ppermute(block, axis, route)


def attend(query_dev, grad_dev, slot_keys, slot_values, slot_ok, head_key, head_value, factor):
    score_slot = (
        jnp.einsum("bhqe,bshke->bhqsk", query_dev, slot_keys, preferred_element_type=jnp.float32)
        * factor
    )
    score_slot = jnp.where(slot_ok[:, None, None, :, :], score_slot, NEG_SCORE)
    score_head = (
        jnp.einsum("bhqe,bhre->bhqr", query_dev, head_key, preferred_element_type=jnp.float32)
        * factor
    )
    top = jnp.maximum(jnp.max(score_slot, axis=(3, 4)), jnp.max(score_head, axis=3))
    total = jnp.sum(jnp.exp(score_slot - top[..., None, None]), axis=(3, 4)) + jnp.sum(
        jnp.exp(score_head - top[..., None]), axis=3
    )
    level = top + jnp.log(total)
    prob_slot = jnp.exp(score_slot - level[..., None, None])
    prob_head = jnp.exp(score_head - level[..., None])
    low_slot = prob_slot.astype(jnp.bfloat16)
    low_head = prob_head.astype(jnp.bfloat16)
    attended = jnp.einsum(
        "bhqsk,bshke->bhqe", low_slot, slot_values, preferred_element_type=jnp.float32
    )
    attended = attended + jnp.einsum(
        "bhqr,bhre->bhqe", low_head, head_value, preferred_element_type=jnp.float32
    )
    delta = jnp.sum(grad_dev.astype(jnp.float32) * attended, axis=-1)
    dprob_slot = jnp.einsum(
        "bhqe,bshke->bhqsk", grad_dev, slot_values, preferred_element_type=jnp.float32
    )
    dprob_head = jnp.einsum(
        "bhqe,bhre->bhqr", grad_dev, head_value, preferred_element_type=jnp.float32
    )
    mix_slot = (factor * prob_slot * (dprob_slot - delta[..., None, None])).astype(jnp.bfloat16)
    mix_head = (factor * prob_head * (dprob_head - delta[..., None])).astype(jnp.bfloat16)
    q_grad = jnp.einsum(
        "bhqsk,bshke->bhqe", mix_slot, slot_keys, preferred_element_type=jnp.float32
    )
    q_grad = q_grad + jnp.einsum(
        "bhqr,bhre->bhqe", mix_head, head_key, preferred_element_type=jnp.float32
    )
    return (q_grad, mix_slot, low_slot, mix_head, low_head)


def body(
    queries,
    key_rows,
    value_rows,
    out_grad,
    padding,
    header_keys,
    header_values,
    neighbours,
    slot_valid,
    crystal_ids,
    header_index,
):
    seq_count = lax.axis_size("seq")
    place = lax.axis_index("seq")
    tok_count = queries.shape[0]
    width = queries.shape[1]
    blocks_dev = neighbours.shape[0]
    heads_dev = width // DH
    span = (2 * REACH + 1) * blocks_dev
    all_blocks = blocks_dev * seq_count
    factor = 1.0 / math.sqrt(DH)
    signed_offsets = [offset for offset in range(-REACH, REACH + 1) if offset != 0]
    own = (key_rows, value_rows, padding.astype(jnp.bfloat16))
    pieces = {0: own}
    for offset in signed_offsets:
        pieces[offset] = passed_along((own[0], own[1], own[2]), "seq", -offset)
    ordered = [pieces[offset] for offset in range(-REACH, REACH + 1)]
    win_key = jnp.concatenate([item[0] for item in ordered], axis=0).reshape(
        span, BLK, heads_dev, DH
    )
    win_value = jnp.concatenate([item[1] for item in ordered], axis=0).reshape(
        span, BLK, heads_dev, DH
    )
    win_pad = jnp.concatenate([item[2] for item in ordered], axis=0).reshape(span, BLK)
    win_key = jnp.transpose(win_key, (0, 2, 1, 3))
    win_value = jnp.transpose(win_value, (0, 2, 1, 3))
    first = (place - REACH) * blocks_dev % all_blocks
    local = (neighbours - first) % all_blocks
    table_key, table_value = (
        lax.all_gather(header_keys, "seq", axis=0, tiled=True),
        lax.all_gather(header_values, "seq", axis=0, tiled=True),
    )
    crystal_count = header_index.shape[0]
    table_rows = table_key.shape[0]
    match = crystal_ids[:, None, None] == jnp.arange(crystal_count, dtype=jnp.int32)[None, :, None]
    rows = jnp.sum(jnp.where(match, header_index[None, :, :], 0), axis=1).reshape(-1)
    pick = (rows[:, None] == jnp.arange(table_rows, dtype=jnp.int32)[None, :]).astype(jnp.bfloat16)
    head_key = jnp.dot(pick, table_key, preferred_element_type=jnp.float32).astype(jnp.bfloat16)
    head_value = jnp.dot(pick, table_value, preferred_element_type=jnp.float32).astype(jnp.bfloat16)
    head_key = jnp.transpose(head_key.reshape(blocks_dev, 2, heads_dev, DH), (0, 2, 1, 3))
    head_value = jnp.transpose(head_value.reshape(blocks_dev, 2, heads_dev, DH), (0, 2, 1, 3))
    slot_keys = jnp.take(win_key, local, axis=0)
    slot_values = jnp.take(win_value, local, axis=0)
    slot_ok = (jnp.take(win_pad, local, axis=0) > 0) & (slot_valid[:, :, None] > 0)
    query_dev = jnp.transpose(queries.reshape(blocks_dev, BLK, heads_dev, DH), (0, 2, 1, 3))
    grad_dev = jnp.transpose(out_grad.reshape(blocks_dev, BLK, heads_dev, DH), (0, 2, 1, 3))
    q_grad, mix_slot, low_slot, mix_head, low_head = attend(
        query_dev, grad_dev, slot_keys, slot_values, slot_ok, head_key, head_value, factor
    )
    onehot = (local[:, :, None] == jnp.arange(span, dtype=jnp.int32)[None, None, :]).astype(
        jnp.bfloat16
    )

    def to_window(weights, other):
        spread = jnp.einsum(
            "bsw,bhqsk->bhqwk", onehot, weights, preferred_element_type=jnp.float32
        ).astype(jnp.bfloat16)
        merged = jnp.einsum("bhqwk,bhqe->wkhe", spread, other, preferred_element_type=jnp.float32)
        return merged.reshape(span * BLK, width).astype(jnp.bfloat16)

    win_key_grad = to_window(mix_slot, query_dev)
    win_value_grad = to_window(low_slot, grad_dev)
    centre = REACH * tok_count
    own_key, own_value = lax.optimization_barrier(
        (win_key_grad[centre : centre + tok_count], win_value_grad[centre : centre + tok_count])
    )
    key_sum = own_key.astype(jnp.float32)
    value_sum = own_value.astype(jnp.float32)
    for offset in signed_offsets:
        start = (offset + REACH) * tok_count
        back_key, back_value = passed_along(
            (win_key_grad[start : start + tok_count], win_value_grad[start : start + tok_count]),
            "seq",
            offset,
        )
        key_sum = key_sum + back_key.astype(jnp.float32)
        value_sum = value_sum + back_value.astype(jnp.float32)
    pick_wide = pick.astype(jnp.float32)
    head_key_grad = jnp.einsum(
        "bhqr,bhqe->brhe", mix_head, query_dev, preferred_element_type=jnp.float32
    ).reshape(blocks_dev * 2, width)
    head_value_grad = jnp.einsum(
        "bhqr,bhqe->brhe", low_head, grad_dev, preferred_element_type=jnp.float32
    ).reshape(blocks_dev * 2, width)
    table_key_grad = jnp.dot(pick_wide.T, head_key_grad, precision=lax.Precision.HIGHEST)
    table_value_grad = jnp.dot(pick_wide.T, head_value_grad, precision=lax.Precision.HIGHEST)
    owned_key_grad, owned_value_grad = (
        lax.psum_scatter(table_key_grad, "seq", scatter_dimension=0, tiled=True),
        lax.psum_scatter(table_value_grad, "seq", scatter_dimension=0, tiled=True),
    )
    q_out = jnp.transpose(q_grad, (0, 2, 1, 3)).reshape(tok_count, width).astype(jnp.bfloat16)
    q_final, k_final, v_final = (
        lax.all_to_all(q_out, "head", split_axis=0, concat_axis=1, tiled=True),
        lax.all_to_all(
            key_sum.astype(jnp.bfloat16), "head", split_axis=0, concat_axis=1, tiled=True
        ),
        lax.all_to_all(
            value_sum.astype(jnp.bfloat16), "head", split_axis=0, concat_axis=1, tiled=True
        ),
    )
    return (
        q_final,
        k_final,
        v_final,
        owned_key_grad.astype(jnp.bfloat16),
        owned_value_grad.astype(jnp.bfloat16),
    )


def solution(mesh):
    in_specs = (
        P("seq", "head"),
        P("seq", "head"),
        P("seq", "head"),
        P("seq", "head"),
        P("seq"),
        P("seq", "head"),
        P("seq", "head"),
        P("seq", None),
        P("seq", None),
        P("seq"),
        P(),
    )
    out_specs = (
        P(("seq", "head"), None),
        P(("seq", "head"), None),
        P(("seq", "head"), None),
        P("seq", "head"),
        P("seq", "head"),
    )
    return jax.shard_map(body, mesh=mesh, in_specs=in_specs, out_specs=out_specs, check_vma=False)
```

profile of v0, /device:TPU:8, one launch (start us, length us, event | category | flops | bytes accessed | tf_op | source)
XLA Modules:
  0.0 2404.1 jit_solution(14321525322619161565)
XLA Ops:
  1.4 4.5 collective-permute-start
  7.8 12.8 collective-permute-start.2
  26.4 391.1 %all-gather = bf16[256,1,1024]{2,1,0:T(2,128)(2,1)S(1)} all-gather(bf16[1,1,1024]{2,1,0:T(2,128)(2,1)} %bitcast.269), channel_id=1, replica_groups=mesh['seq'=256,'head'=2] {'seq'}, dimensions={0}, use_global_device_ids=true | all-gather | bytes 526336 | tf_op jit(solution)/shard_map/all_gather | solution.py:105
  419.6 371.1 %all-gather.1 = bf16[256,1,1024]{2,1,0:T(2,128)(2,1)S(1)} all-gather(bf16[1,1,1024]{2,1,0:T(2,128)(2,1)S(1)} %bitcast.270), channel_id=1, replica_groups=mesh['seq'=256,'head'=2] {'seq'}, dimensions={0}, use_global_device_ids=true | all-gather | bytes 526336 | tf_op jit(solution)/shard_map/all_gather | solution.py:106
  794.3 4.1 collective-permute-start.3
  803.9 4.8 collective-permute-start.4
  812.5 10.0 collective-permute-start.6
  823.6 12.8 collective-permute-done.10
  836.4 7.3 collective-permute-start.7
  843.7 5.6 collective-permute-done.11
  860.0 12.5 collective-permute-done.7
  891.6 6.2 copy.189
  897.8 5.4 copy.193
  907.2 5.2 all-to-all-start
  912.4 4.7 convert_bitcast_fusion.1
  928.3 10.0 collective-permute-start.13
  939.6 4.5 collective-permute-start.12
  961.2 10.0 collective-permute-start.17
  971.2 6.2 collective-permute-start.16
  987.8 4.2 collective-permute-done.18
  992.0 8.2 collective-permute-done.17
  1000.2 7.8 collective-permute-done.16
  1010.9 6.0 all-to-all-start.2
  1016.9 1378.6 %all-reduce.4 = (bf16[256,1024]{1,0:T(8,128)(2,1)}, bf16[256,1024]{1,0:T(8,128)(2,1)}) all-reduce(f32[256,1024]{1,0:T(8,128)S(1)} %fusion.53, f32[256,1024]{1,0:T(8,128)S(1)} %fusion.50), channel_id=2, replica_groups=mesh['seq'=256,'head'=2] {'seq'}, use_global_device_ids=true, to_apply=%region_6.8.clone | all-reduce | flops 524288 | bytes 3145728
  (148 shorter events, 109.0 us)
Async XLA Ops:
  1.4 792.9 %collective-permute-start = (bf16[256]{0:T(256)(128)(2,1)S(1)}, bf16[256]{0:T(256)(128)(2,1)S(1)}, u32[]{:S(2)}, u32[]{:S(2)}) collective-permute-start(bf16[256]{0:T(256)(128)(2,1)S(1)} %convert_element_type.105), channel_id=1, source_target_pairs={{508,0},{510,2},{0,4},{2,6},{4,8},{6,10},{8,12},{10,14},{12,16},{1... | collective-permute-start | bytes 1544 | tf_op jit(solution)/shard_map/ppermute | solution.py:19
  5.9 794.2 %collective-permute-start.1 = (bf16[256]{0:T(256)(128)(2,1)S(1)}, bf16[256]{0:T(256)(128)(2,1)S(1)}, u32[]{:S(2)}, u32[]{:S(2)}) collective-permute-start(bf16[256]{0:T(256)(128)(2,1)S(1)} %convert_element_type.105), channel_id=1, source_target_pairs={{510,0},{0,2},{2,4},{4,6},{6,8},{8,10},{10,12},{12,14},{14,16},{16... | collective-permute-start | bytes 1544 | tf_op jit(solution)/shard_map/ppermute | solution.py:19
  7.8 794.2 %collective-permute-start.2 = (bf16[256]{0:T(256)(128)(2,1)S(1)}, bf16[256]{0:T(256)(128)(2,1)S(1)}, u32[]{:S(2)}, u32[]{:S(2)}) collective-permute-start(bf16[256]{0:T(256)(128)(2,1)S(1)} %convert_element_type.105), channel_id=1, source_target_pairs={{2,0},{4,2},{6,4},{8,6},{10,8},{12,10},{14,12},{16,14},{18,16},{20... | collective-permute-start | bytes 1544 | tf_op jit(solution)/shard_map/ppermute | solution.py:19
  20.6 788.9 %collective-permute-start.8 = (bf16[256,1024]{1,0:T(8,128)(2,1)}, bf16[256,1024]{1,0:T(8,128)(2,1)}, u32[]{:S(2)}, u32[]{:S(2)}) collective-permute-start(bf16[256,1024]{1,0:T(8,128)(2,1)} %param.15), channel_id=1, source_target_pairs={{508,0},{510,2},{0,4},{2,6},{4,8},{6,10},{8,12},{10,14},{12,16},{1... | collective-permute-start | bytes 1572872 | tf_op jit(solution)/shard_map/ppermute | solution.py:19
  22.5 789.9 %collective-permute-start.9 = (bf16[256,1024]{1,0:T(8,128)(2,1)}, bf16[256,1024]{1,0:T(8,128)(2,1)}, u32[]{:S(2)}, u32[]{:S(2)}) collective-permute-start(bf16[256,1024]{1,0:T(8,128)(2,1)} %param.15), channel_id=1, source_target_pairs={{510,0},{0,2},{2,4},{4,6},{6,8},{8,10},{10,12},{12,14},{14,16},{16... | collective-permute-start | bytes 1572872 | tf_op jit(solution)/shard_map/ppermute | solution.py:19
  26.4 766.1 %copy-start.2 = (bf16[32,8,8,128]{3,2,1,0:T(8,128)(2,1)}, bf16[32,8,8,128]{3,2,1,0:T(8,128)(2,1)S(1)}, u32[]{:S(2)}) copy-start(bf16[32,8,8,128]{3,2,1,0:T(8,128)(2,1)S(1)} %copy.246) | copy-start | bytes 1572868
  794.3 9.6 collective-permute-start.3
  800.1 36.4 %collective-permute-start.10 = (bf16[256,1024]{1,0:T(8,128)(2,1)S(1)}, bf16[256,1024]{1,0:T(8,128)(2,1)S(1)}, u32[]{:S(2)}, u32[]{:S(2)}) collective-permute-start(bf16[256,1024]{1,0:T(8,128)(2,1)S(1)} %copy-done.9), channel_id=1, source_target_pairs={{2,0},{4,2},{6,4},{8,6},{10,8},{12,10},{14,12},{16,14},{18,16},{20... | collective-permute-start | bytes 1572872 | tf_op jit(solution)/shard_map/ppermute | solution.py:19
  802.0 47.4 %collective-permute-start.11 = (bf16[256,1024]{1,0:T(8,128)(2,1)S(1)}, bf16[256,1024]{1,0:T(8,128)(2,1)S(1)}, u32[]{:S(2)}, u32[]{:S(2)}) collective-permute-start(bf16[256,1024]{1,0:T(8,128)(2,1)S(1)} %copy-done.9), channel_id=1, source_target_pairs={{4,0},{6,2},{8,4},{10,6},{12,8},{14,10},{16,12},{18,14},{20,16},{2... | collective-permute-start | bytes 1572872 | tf_op jit(solution)/shard_map/ppermute | solution.py:19
  803.9 49.4 %collective-permute-start.4 = (bf16[256,1024]{1,0:T(8,128)(2,1)}, bf16[256,1024]{1,0:T(8,128)(2,1)}, u32[]{:S(2)}, u32[]{:S(2)}) collective-permute-start(bf16[256,1024]{1,0:T(8,128)(2,1)} %param.14), channel_id=1, source_target_pairs={{508,0},{510,2},{0,4},{2,6},{4,8},{6,10},{8,12},{10,14},{12,16},{1... | collective-permute-start | bytes 1572872 | tf_op jit(solution)/shard_map/ppermute | solution.py:19
  809.5 44.9 %collective-permute-start.5 = (bf16[256,1024]{1,0:T(8,128)(2,1)}, bf16[256,1024]{1,0:T(8,128)(2,1)}, u32[]{:S(2)}, u32[]{:S(2)}) collective-permute-start(bf16[256,1024]{1,0:T(8,128)(2,1)} %param.14), channel_id=1, source_target_pairs={{510,0},{0,2},{2,4},{4,6},{6,8},{8,10},{10,12},{12,14},{14,16},{16... | collective-permute-start | bytes 1572872 | tf_op jit(solution)/shard_map/ppermute | solution.py:19
  812.5 46.5 %collective-permute-start.6 = (bf16[256,1024]{1,0:T(8,128)(2,1)}, bf16[256,1024]{1,0:T(8,128)(2,1)}, u32[]{:S(2)}, u32[]{:S(2)}) collective-permute-start(bf16[256,1024]{1,0:T(8,128)(2,1)} %param.14), channel_id=1, source_target_pairs={{2,0},{4,2},{6,4},{8,6},{10,8},{12,10},{14,12},{16,14},{18,16},{20... | collective-permute-start | bytes 1572872 | tf_op jit(solution)/shard_map/ppermute | solution.py:19
  836.4 36.1 %collective-permute-start.7 = (bf16[256,1024]{1,0:T(8,128)(2,1)}, bf16[256,1024]{1,0:T(8,128)(2,1)}, u32[]{:S(2)}, u32[]{:S(2)}) collective-permute-start(bf16[256,1024]{1,0:T(8,128)(2,1)} %param.14), channel_id=1, source_target_pairs={{4,0},{6,2},{8,4},{10,6},{12,8},{14,10},{16,12},{18,14},{20,16},{2... | collective-permute-start | bytes 1572872 | tf_op jit(solution)/shard_map/ppermute | solution.py:19
  907.2 75.3 %all-to-all-start = ((bf16[2,128,1024]{1,2,0:T(8,128)(2,1)}), bf16[2,128,1024]{1,2,0:T(8,128)(2,1)}, u32[]{:S(2)}, u32[]{:S(2)}) async-start(bf16[2,128,1024]{1,2,0:T(8,128)(2,1)} %bitcast.29), calls=%async_computation | async-start | bytes 1048576 | tf_op jit(solution)/shard_map/all_to_all | solution.py:168
  920.7 38.5 %collective-permute-start.15 = (bf16[256,1024]{1,0:T(8,128)(2,1)}, bf16[256,1024]{1,0:T(8,128)(2,1)}, u32[]{:S(2)}, u32[]{:S(2)}) collective-permute-start(bf16[256,1024]{1,0:T(8,128)(2,1)} %bitcast.222), channel_id=1, source_target_pairs={{508,0},{510,2},{0,4},{2,6},{4,8},{6,10},{8,12},{10,14},{12,16},{1... | collective-permute-start | bytes 1572872 | tf_op jit(solution)/shard_map/ppermute | solution.py:19
  925.1 36.1 %collective-permute-start.14 = (bf16[256,1024]{1,0:T(8,128)(2,1)}, bf16[256,1024]{1,0:T(8,128)(2,1)}, u32[]{:S(2)}, u32[]{:S(2)}) collective-permute-start(bf16[256,1024]{1,0:T(8,128)(2,1)} %bitcast.223), channel_id=1, source_target_pairs={{510,0},{0,2},{2,4},{4,6},{6,8},{8,10},{10,12},{12,14},{14,16},{16... | collective-permute-start | bytes 1572872 | tf_op jit(solution)/shard_map/ppermute | solution.py:19
  928.3 42.8 %collective-permute-start.13 = (bf16[256,1024]{1,0:T(8,128)(2,1)}, bf16[256,1024]{1,0:T(8,128)(2,1)}, u32[]{:S(2)}, u32[]{:S(2)}) collective-permute-start(bf16[256,1024]{1,0:T(8,128)(2,1)} %bitcast.224), channel_id=1, source_target_pairs={{2,0},{4,2},{6,4},{8,6},{10,8},{12,10},{14,12},{16,14},{18,16},{20... | collective-permute-start | bytes 1572872 | tf_op jit(solution)/shard_map/ppermute | solution.py:19
  939.6 40.2 %collective-permute-start.12 = (bf16[256,1024]{1,0:T(8,128)(2,1)}, bf16[256,1024]{1,0:T(8,128)(2,1)}, u32[]{:S(2)}, u32[]{:S(2)}) collective-permute-start(bf16[256,1024]{1,0:T(8,128)(2,1)} %bitcast.225), channel_id=1, source_target_pairs={{4,0},{6,2},{8,4},{10,6},{12,8},{14,10},{16,12},{18,14},{20,16},{2... | collective-permute-start | bytes 1572872 | tf_op jit(solution)/shard_map/ppermute | solution.py:19
  951.9 35.9 %collective-permute-start.19 = (bf16[256,1024]{1,0:T(8,128)(2,1)}, bf16[256,1024]{1,0:T(8,128)(2,1)}, u32[]{:S(2)}, u32[]{:S(2)}) collective-permute-start(bf16[256,1024]{1,0:T(8,128)(2,1)} %bitcast.218), channel_id=1, source_target_pairs={{508,0},{510,2},{0,4},{2,6},{4,8},{6,10},{8,12},{10,14},{12,16},{1... | collective-permute-start | bytes 1572872 | tf_op jit(solution)/shard_map/ppermute | solution.py:19
  959.2 32.8 %collective-permute-start.18 = (bf16[256,1024]{1,0:T(8,128)(2,1)}, bf16[256,1024]{1,0:T(8,128)(2,1)}, u32[]{:S(2)}, u32[]{:S(2)}) collective-permute-start(bf16[256,1024]{1,0:T(8,128)(2,1)} %bitcast.219), channel_id=1, source_target_pairs={{510,0},{0,2},{2,4},{4,6},{6,8},{8,10},{10,12},{12,14},{14,16},{16... | collective-permute-start | bytes 1572872 | tf_op jit(solution)/shard_map/ppermute | solution.py:19
  961.2 39.0 %collective-permute-start.17 = (bf16[256,1024]{1,0:T(8,128)(2,1)}, bf16[256,1024]{1,0:T(8,128)(2,1)}, u32[]{:S(2)}, u32[]{:S(2)}) collective-permute-start(bf16[256,1024]{1,0:T(8,128)(2,1)} %bitcast.220), channel_id=1, source_target_pairs={{2,0},{4,2},{6,4},{8,6},{10,8},{12,10},{14,12},{16,14},{18,16},{20... | collective-permute-start | bytes 1572872 | tf_op jit(solution)/shard_map/ppermute | solution.py:19
  971.2 36.8 %collective-permute-start.16 = (bf16[256,1024]{1,0:T(8,128)(2,1)}, bf16[256,1024]{1,0:T(8,128)(2,1)}, u32[]{:S(2)}, u32[]{:S(2)}) collective-permute-start(bf16[256,1024]{1,0:T(8,128)(2,1)} %bitcast.221), channel_id=1, source_target_pairs={{4,0},{6,2},{8,4},{10,6},{12,8},{14,10},{16,12},{18,14},{20,16},{2... | collective-permute-start | bytes 1572872 | tf_op jit(solution)/shard_map/ppermute | solution.py:19
  982.5 28.4 %all-to-all-start.1 = ((bf16[2,128,1024]{2,1,0:T(8,128)(2,1)}), bf16[2,128,1024]{2,1,0:T(8,128)(2,1)S(1)}, u32[]{:S(2)}, u32[]{:S(2)}) async-start(bf16[2,128,1024]{2,1,0:T(8,128)(2,1)} %bitcast.47), calls=%async_computation.1 | async-start | bytes 1048576 | tf_op jit(solution)/shard_map/all_to_all | solution.py:169
  1010.9 1391.7 %all-to-all-start.2 = ((bf16[2,128,1024]{2,1,0:T(8,128)(2,1)}), bf16[2,128,1024]{2,1,0:T(8,128)(2,1)S(1)}, u32[]{:S(2)}, u32[]{:S(2)}) async-start(bf16[2,128,1024]{2,1,0:T(8,128)(2,1)} %bitcast.260), calls=%async_computation.2 | async-start | bytes 1048576 | tf_op jit(solution)/shard_map/all_to_all | solution.py:172
  (12 other events, 1296.1 us)
where the time goes:
time: 2410 us; the launch traced here: 2400 us
  blocking collectives  2140 us (89%)
  starting transfers between devices  110 us (5%)
  waiting for transfers between devices  57.1 us (2%)
  local copies, waits for them, and re-layouts  56 us (2%)
  matrix products  24.5 us (1%)
    unnamed x1, blocking collectives  1380 us
    all_gather x1, blocking collectives, body(): lax.all_gather(header_keys, 'seq', axis=0, tiled=True)  391 us
    all_gather x1, blocking collectives, body(): lax.all_gather(header_values, 'seq', axis=0, tiled=True)  371 us
    ppermute x20, starting transfers between devices, passed_along(): return lax.ppermute(block, axis, route)  95.1 us
    ppermute x20, waiting for transfers between devices, passed_along(): return lax.ppermute(block, axis, route)  56.9 us
  transfers between devices with their start and end apart: 23, of which 10 were waited for; matrix products, arithmetic and copies ran while one was open for 2% of the time, Pallas kernels for 0%

commit v1 on v0

v1 whole, which is shorter than its diff:
```python
import math

import jax
import jax.numpy as jnp
from jax import lax
from jax.experimental import pallas as pl
from jax.experimental.pallas import tpu as pltpu
from jax.sharding import PartitionSpec as P

DH = 128
BLK = 128
NEG = -1e30
FACTOR = 1.0 / math.sqrt(DH)
F32 = jnp.float32
BF16 = jnp.bfloat16
HD = 4
WIN = 1024
KEYS = WIN + 16
HROW = 512
SEQ = 256


def kernel(
    q_in, g_in, k_in, v_in, meta_in, hdr_in, hidx,
    q_out, k_out, v_out, h_out,
    qg, kv, bias, probs, mixes, grads, back, meta, meta_s, table, hb, hd, htab, rz, sz, rx, sx, ry,
    f_send, f_recv, own_sem, b_send, b_recv, bown_sem, m_send, m_recv, ms_sem,
    hs_send, hs_recv, ht_send, ht_recv,
):
    e = lax.axis_index("seq")
    h = lax.axis_index("head")
    core = lax.rem(e, 2)
    chip = e // 2
    j8 = lax.rem(e, 8)
    x4 = lax.rem(e // 8, 4)
    z8 = e // 32

    def wrap(index):
        return lax.rem(index + SEQ, SEQ)

    step = 2 * core - 1
    peer = e + 1 - 2 * core
    near = wrap(e + step)
    far = wrap(e + 2 * step)
    far_from = wrap(e - 2 * step)
    after = wrap(2 * chip + 2)
    before = wrap(2 * chip - 1)

    def y_peer(d):
        return e - j8 + lax.rem(j8 + d, 8)

    def x_peer(d):
        return e - 8 * x4 + 8 * lax.rem(x4 + d, 4)

    def z_peer(d):
        return e - 32 * z8 + 32 * lax.rem(z8 + d, 8)

    barrier = pltpu.get_barrier_semaphore()

    def greet(device, other):
        pl.semaphore_signal(barrier, inc=1, device_id=(device, other), device_id_type=pl.DeviceIdType.MESH)

    for d in range(1, 8):
        greet(y_peer(d), h)
        greet(z_peer(d), h)
    for d in range(1, 4):
        greet(x_peer(d), h)
    greet(near, h)
    greet(far_from, h)
    greet(e, 1 - h)
    greet(peer, 1 - h)
    next_chip = wrap(2 * (chip + step))
    for other in range(2):
        greet(next_chip, other)
        greet(next_chip + 1, other)

    def remote(src, dst, send, recv, device, other):
        return pltpu.make_async_remote_copy(
            src_ref=src, dst_ref=dst, send_sem=send, recv_sem=recv,
            device_id=(device, other), device_id_type=pl.DeviceIdType.MESH,
        )

    table[pl.ds(e, 1)] = hdr_in[...][None]
    meta[pl.ds(1 + core, 1)] = meta_in[...][None]

    pl.semaphore_wait(barrier, 25)

    def row_y(d):
        return remote(table.at[e], table.at[e], hs_send.at[d - 1], hs_recv.at[d - 1], y_peer(d), h)

    def row_x(d):
        part = table.at[pl.ds(e - j8, 8)]
        return remote(part, part, hs_send.at[6 + d], hs_recv.at[6 + d], x_peer(d), h)

    def row_z(d):
        part = table.at[pl.ds(32 * z8, 32)]
        return remote(part, part, hs_send.at[9 + d], hs_recv.at[9 + d], z_peer(d), h)

    for d in range(1, 8):
        row_y(d).start()

    ext_slot = 3 - 3 * core
    targets = ((peer, 1 - core, 1 + core), (near, 1 - core, ext_slot), (far, core, ext_slot))

    def meta_copy(kind):
        device, _, slot = targets[kind]
        return remote(meta.at[1 + core], meta.at[slot], m_send.at[kind], m_recv.at[kind], device, h)

    for kind in range(3):
        meta_copy(kind).start()

    def key_row(slot):
        return pl.multiple_of(slot * 256 + 16 * (slot // 2), 16)

    def place(array, head, slot):
        if array < 2:
            return qg.at[head, array, pl.ds(pl.multiple_of(slot * 256, 256), 256)]
        return kv.at[head, array - 2, pl.ds(key_row(slot), 256)]

    ins = (q_in, g_in, k_in, v_in)

    def forward(kind, array, head):
        device, group, slot = targets[kind]
        cols = pl.ds(pl.multiple_of((group * HD + head) * DH, DH), DH)
        return remote(
            ins[array].at[:, cols], place(array, head, slot),
            f_send.at[head, kind, array], f_recv.at[head, kind, array], device, h,
        )

    def own_copy(array, head):
        cols = pl.ds(pl.multiple_of((core * HD + head) * DH, DH), DH)
        return pltpu.make_async_copy(ins[array].at[:, cols], place(array, head, 1 + core), own_sem.at[head, array])

    def send_head(head, carry):
        for array in range(4):
            for kind in range(3):
                forward(kind, array, head).start()
            own_copy(array, head).start()
        return carry

    send_head(0, 0)
    for d in range(1, 8):
        row_y(d).wait_recv()
    for d in range(1, 4):
        row_x(d).start()
    for d in range(1, 4):
        row_x(d).wait_recv()
    for d in range(1, 8):
        row_z(d).start()
    lax.fori_loop(1, HD, send_head, 0)

    for kind in range(3):
        meta_copy(kind).wait_recv()
    to_scalar = pltpu.make_async_copy(meta, meta_s, ms_sem)
    to_scalar.start()
    to_scalar.wait()
    id_x = meta_s[1, 2, 0]
    id_y = meta_s[2, 3, 0]
    for pair in range(4):
        ids = jnp.concatenate([meta[pair, 2:3, :], meta[pair, 3:4, :]], axis=1).astype(F32)
        for block in range(8):
            codes = meta[block // 2, block % 2 : block % 2 + 1, :].astype(F32)
            codes = jnp.broadcast_to(codes, (BLK, BLK)).T
            codes = jnp.concatenate([codes, codes], axis=1)
            row = block * BLK + 16 * (block // 4)
            bias[pair, row : row + BLK, :] = jnp.where(codes == ids, 0.0, NEG)
        rows = lax.broadcasted_iota(jnp.int32, (16, 256), 0)
        both = jnp.where(rows < 2, id_x, jnp.where((rows < 4) & (id_x != id_y), id_y, -2))
        bias[pair, HROW : HROW + 16, :] = jnp.where(both.astype(F32) == ids, 0.0, NEG)
    probs[784:1040, 0:256] = jnp.zeros((256, 256), BF16)
    mixes[784:1040, 0:256] = jnp.zeros((256, 256), BF16)
    probs[0:256, 768:1024] = jnp.zeros((256, 256), BF16)
    mixes[0:256, 768:1024] = jnp.zeros((256, 256), BF16)

    for d in range(1, 8):
        row_z(d).wait_recv()
    rows_x = (hidx[2 * id_x], hidx[2 * id_x + 1])
    rows_y = (hidx[2 * id_y], hidx[2 * id_y + 1])
    for slot, row in enumerate(rows_x + rows_y):
        hb[slot] = table[row].astype(F32)
    for head in range(HD):
        for array in range(2):
            at = pl.ds(array * 8 + core * HD + head, 1)
            lines = [hb[slot, at, :] for slot in range(4)] + [jnp.zeros((12, DH), F32)]
            kv[head, array, HROW : HROW + 16, :] = jnp.concatenate(lines, axis=0).astype(BF16)

    mine = 2 * core + h

    def ret(which, head):
        col = pl.ds(pl.multiple_of(h * 1024 + (core * HD + head) * DH, DH), DH)
        if which < 3:
            there = lax.rem(mine + which + 1, 4)
            device, other, block, sem = 2 * chip + there // 2, lax.rem(there, 2), 2 + there, which
            side = 0
        else:
            other = (which - 3) % 2
            block = (6, 7, 0, 1)[which - 3]
            device = after if which < 5 else before
            side = 1
            sem = 3 + mine
        src = grads.at[head, :, pl.ds(block * BLK, BLK), :]
        return remote(src, back.at[side, :, :, col], b_send.at[head, which], b_recv.at[head, sem], device, other)

    def ret_wait(which, head):
        col = pl.ds(pl.multiple_of(h * 1024 + (core * HD + head) * DH, DH), DH)
        src = grads.at[head, :, pl.ds(0, BLK), :]
        dst = back.at[0 if which < 3 else 1, :, :, col]
        remote(src, dst, b_send.at[head, which], b_recv.at[head, which], peer, h).wait_recv()

    def ret_own(head):
        col = pl.ds(pl.multiple_of(h * 1024 + (core * HD + head) * DH, DH), DH)
        src = grads.at[head, :, pl.ds(pl.multiple_of((2 + mine) * BLK, BLK), BLK), :]
        return pltpu.make_async_copy(src, back.at[0, :, :, col], bown_sem.at[head])

    def nt(a, b):
        return lax.dot_general(a, b, (((1,), (1,)), ((), ())), preferred_element_type=F32)

    def work(head, carry):
        for array in range(4):
            for kind in range(3):
                forward(kind, array, head).wait_recv()
            own_copy(array, head).wait()
        for pair in range(4):
            lo, hi = (0, 784) if pair == 0 else (256, KEYS) if pair == 3 else (0, KEYS)
            cols = slice(pair * 256, pair * 256 + 256)
            q = qg[head, 0, cols, :]
            g = qg[head, 1, cols, :]
            keys = kv[head, 0, lo:hi, :]
            values = kv[head, 1, lo:hi, :]
            score = nt(keys, q) * FACTOR + bias[pair, lo:hi, :]
            top = jnp.max(score, axis=0, keepdims=True)
            grown = jnp.exp(score - top)
            prob = grown * (1.0 / jnp.sum(grown, axis=0, keepdims=True))
            low = prob.astype(BF16)
            dprob = nt(values, g)
            delta = jnp.sum(low.astype(F32) * dprob, axis=0, keepdims=True)
            mixing = (FACTOR * prob * (dprob - delta)).astype(BF16)
            probs[lo:hi, cols] = low
            mixes[lo:hi, cols] = mixing
            q_grad = lax.dot_general(mixing, keys, (((0,), (0,)), ((), ())), preferred_element_type=F32)
            grads[head, 0, cols, :] = q_grad.astype(BF16)
        for array, weights in ((1, mixes), (2, probs)):
            total = jnp.dot(weights[...], qg[head, array - 1], preferred_element_type=F32)
            grads[head, array, 0:512, :] = total[0:512].astype(BF16)
            grads[head, array, 512:1024, :] = total[528:1040].astype(BF16)
            for slot in range(4):
                hd[slot, pl.ds((array - 1) * HD + head, 1), :] = total[HROW + slot : HROW + slot + 1]
        for which in range(7):
            ret(which, head).start()
        ret_own(head).start()
        return carry

    lax.fori_loop(0, HD, work, 0)

    home_x = meta_s[1, 4, 0] == chip
    home_y = (meta_s[2, 5, 0] == chip) & (id_x != id_y)
    names = [jnp.where(home_x, row, -1) for row in rows_x] + [jnp.where(home_y, row, -1) for row in rows_y]

    def fill(row, carry):
        total = jnp.zeros((8, DH), F32)
        for slot in range(4):
            total = total + jnp.where(names[slot] == row, hd[slot], 0.0)
        htab[pl.ds(row, 1)] = total[None]
        return carry

    lax.fori_loop(0, SEQ, fill, 0)

    def out_z(d):
        src = htab.at[pl.ds(32 * lax.rem(z8 + d, 8), 32)]
        return remote(src, rz.at[d - 1], ht_send.at[d - 1], ht_recv.at[d - 1], z_peer(d), h)

    def out_x(d):
        src = sz.at[pl.ds(8 * lax.rem(x4 + d, 4), 8)]
        return remote(src, rx.at[d - 1], ht_send.at[6 + d], ht_recv.at[6 + d], x_peer(d), h)

    def out_y(d):
        src = sx.at[lax.rem(j8 + d, 8)]
        return remote(src, ry.at[j8], ht_send.at[9 + d], ht_recv.at[9 + d], y_peer(d), h)

    for d in range(1, 8):
        out_z(d).start()
    for d in range(1, 8):
        out_z(d).wait_recv()
    total = htab[pl.ds(32 * z8, 32)]
    for d in range(7):
        total = total + rz[d]
    sz[...] = total
    for d in range(1, 4):
        out_x(d).start()
    for d in range(1, 4):
        out_x(d).wait_recv()
    total = sz[pl.ds(8 * x4, 8)]
    for d in range(3):
        total = total + rx[d]
    sx[...] = total
    for d in range(1, 8):
        out_y(d).start()
    ry[pl.ds(j8, 1)] = sx[pl.ds(j8, 1)]
    for d in range(1, 8):
        out_y(d).wait_recv()
    halves = [ry[c] + ry[c + 2] + ry[c + 4] + ry[c + 6] for c in range(2)]
    lines = [halves[0][0:4], halves[1][0:4], halves[0][4:8], halves[1][4:8]]
    h_out[...] = jnp.concatenate(lines, axis=0).astype(BF16)

    def settle(head, carry):
        for which in range(7):
            ret_wait(which, head)
        ret_own(head).wait()
        return carry

    lax.fori_loop(0, HD, settle, 0)
    here = meta_s[1 + core, 4 + h, 0] == chip
    for array, out in ((0, q_out), (1, k_out), (2, v_out)):
        out[...] = jnp.where(here, back[0, array], back[1, array])

    def drain(head, carry):
        for array in range(4):
            for kind in range(3):
                forward(kind, array, head).wait_send()
        for which in range(7):
            ret(which, head).wait_send()
        return carry

    lax.fori_loop(0, HD, drain, 0)
    for kind in range(3):
        meta_copy(kind).wait_send()
    for d in range(1, 8):
        row_y(d).wait_send()
        row_z(d).wait_send()
        out_y(d).wait_send()
        out_z(d).wait_send()
    for d in range(1, 4):
        row_x(d).wait_send()
        out_x(d).wait_send()


def body(
    queries, key_rows, value_rows, out_grad, padding, header_keys, header_values,
    neighbours, slot_valid, crystal_ids, header_index,
):
    used = slot_valid > 0
    size = jnp.sum(used.astype(jnp.int32), axis=1)
    start = jnp.min(jnp.where(used, neighbours, 1 << 20), axis=1)
    first = start // 4
    left = jnp.minimum(4 * first + 4 - start, size)
    home = first + ((left < size) & (left <= 2)).astype(jnp.int32)
    ids = crystal_ids[:, None]
    codes = jnp.where(padding.reshape(2, BLK) > 0, ids, -1)
    wide = (2, BLK)
    meta = jnp.concatenate(
        [codes, jnp.broadcast_to(ids, wide), jnp.broadcast_to(home[:, None], wide), jnp.zeros(wide, jnp.int32)]
    )
    hdr = jnp.concatenate([header_keys.reshape(8, DH), header_values.reshape(8, DH)])
    grad = jax.ShapeDtypeStruct((BLK, 2048), BF16)
    vmem = pl.BlockSpec(memory_space=pltpu.VMEM)
    hbm = pl.BlockSpec(memory_space=pl.ANY)
    dma = pltpu.SemaphoreType.DMA
    q_grad, k_grad, v_grad, h_grad = pl.pallas_call(
        kernel,
        out_shape=(grad, grad, grad, jax.ShapeDtypeStruct((16, DH), BF16)),
        in_specs=[hbm] * 4 + [vmem] * 2 + [pl.BlockSpec(memory_space=pltpu.SMEM)],
        out_specs=[vmem] * 4,
        scratch_shapes=[
            pltpu.VMEM((HD, 2, WIN, DH), BF16),
            pltpu.VMEM((HD, 2, KEYS, DH), BF16),
            pltpu.VMEM((4, KEYS, 256), F32),
            pltpu.VMEM((KEYS, WIN), BF16),
            pltpu.VMEM((KEYS, WIN), BF16),
            pltpu.VMEM((HD, 3, WIN, DH), BF16),
            pltpu.VMEM((2, 3, BLK, 2048), BF16),
            pltpu.VMEM((4, 8, BLK), jnp.int32),
            pltpu.SMEM((4, 8, BLK), jnp.int32),
            pltpu.VMEM((SEQ, 16, DH), BF16),
            pltpu.VMEM((4, 16, DH), F32),
            pltpu.VMEM((4, 8, DH), F32),
            pltpu.VMEM((SEQ, 8, DH), F32),
            pltpu.VMEM((7, 32, 8, DH), F32),
            pltpu.VMEM((32, 8, DH), F32),
            pltpu.VMEM((3, 8, 8, DH), F32),
            pltpu.VMEM((8, 8, DH), F32),
            pltpu.VMEM((8, 8, DH), F32),
            dma((HD, 3, 4)),
            dma((HD, 3, 4)),
            dma((HD, 4)),
            dma((HD, 7)),
            dma((HD, 7)),
            dma((HD,)),
            dma((3,)),
            dma((3,)),
            dma,
            dma((17,)),
            dma((17,)),
            dma((17,)),
            dma((17,)),
        ],
        compiler_params=pltpu.CompilerParams(
            collective_id=0, has_side_effects=True, vmem_limit_bytes=56 * 1024 * 1024
        ),
    )(queries, out_grad, key_rows, value_rows, meta, hdr, header_index.reshape(-1))
    return (q_grad, k_grad, v_grad, h_grad[:8].reshape(1, 1024), h_grad[8:].reshape(1, 1024))


def solution(mesh):
    in_specs = (
        P("seq", "head"),
        P("seq", "head"),
        P("seq", "head"),
        P("seq", "head"),
        P("seq"),
        P("seq", "head"),
        P("seq", "head"),
        P("seq", None),
        P("seq", None),
        P("seq"),
        P(),
    )
    out_specs = (
        P(("seq", "head"), None),
        P(("seq", "head"), None),
        P(("seq", "head"), None),
        P("seq", "head"),
        P("seq", "head"),
    )
    return jax.shard_map(body, mesh=mesh, in_specs=in_specs, out_specs=out_specs, check_vma=False)
```

time: 2410 us -> 146 us (0.06)
  the two profiles are of different devices: /device:TPU:8 before, /device:TPU:7 now
where the time goes in v1:
time: 146 us; the launch traced here: 145 us
  Pallas kernels  134 us (92%)
  local copies, waits for them, and re-layouts  8.37 us (6%)
  other arithmetic  1.54 us (1%)
    pallas_call x1, Pallas kernels, body(): pl.pallas_call(kernel, out_shape=(grad, grad, grad, jax.ShapeDtypeStruct(...  134 us
    unnamed x25, local copies, waits for them, and re-layouts  6.13 us

profile of v1, /device:TPU:7, one launch (start us, length us, event | category | flops | bytes accessed | tf_op | source)
XLA Modules:
  0.0 145.0 jit_solution(17602719276045510742)
XLA Ops:
  0.6 0.0 copy-start.9
  0.6 0.0 copy-start.8
  0.7 0.8 broadcast_in_dim.26
  1.4 0.0 copy-done.8
  1.4 0.1 bitcast_select_fusion
  1.5 0.1 pad.5.clone
  1.6 0.6 copy-done.7
  2.2 0.0 copy-done.6
  2.2 0.1 select_reduce_fusion
  2.4 0.0 copy-start.3
  2.4 0.1 pad.4.clone
  2.5 0.7 add_add_fusion.meta_in
  3.2 0.7 copy-done.4
  3.8 0.6 pad_maximum_fusion.hdr_in
  4.4 0.1 copy-done.5
  4.5 0.1 copy.16
  4.6 0.7 reshape.59.hidx
  5.3 134.4 %shard_map.146 = (bf16[128,2048]{1,0:T(8,128)(2,1)}, bf16[128,2048]{1,0:T(8,128)(2,1)}, bf16[128,2048]{1,0:T(8,128)(2,1)}, bf16[16,128]{1,0:T(8,128)(2,1)}) custom-call(bf16[256,1024]{1,0:T(8,128)(2,1)} %q_in.1, bf16[256,1024]{1,0:T(8,128)(2,1)} %g_in.1, bf16[256,1024]{1,0:T(8,128)(2,1)} %k_in.1, bf16[256,1024]{1,0:T(8,128)(2,1)} %v_in.1, ...), custom_call_target="tpu_custom_call" | custom-call | tf_op jit(solution)/shard_map/pallas_call | solution.py:358
  139.8 0.7 copy-done.2
  140.4 0.6 copy_bitcast_fusion
  141.1 1.9 %copy.24 = bf16[128,2048]{1,0:T(8,128)(2,1)} copy(bf16[128,2048]{1,0:T(8,128)(2,1)} %get-tuple-element.24) | data formatting | bytes 1048576
  143.0 0.8 copy.25
  143.8 0.4 copy-done
  144.2 0.8 copy.26
  (15 shorter events, 0.1 us)
Async XLA Ops:
  0.6 0.8 copy-start.9
  0.6 0.8 copy-start.8
  1.5 0.7 copy-start.7
  1.5 0.7 copy-start.6
  2.4 0.8 copy-start.3
  3.1 0.7 copy-start.4
  3.8 0.7 copy-start.5
  139.8 0.7 copy-start.2
  141.1 1.9 %copy-start.1 = (bf16[128,2048]{1,0:T(8,128)(2,1)S(1)}, bf16[128,2048]{1,0:T(8,128)(2,1)}, u32[]{:S(2)}) copy-start(bf16[128,2048]{1,0:T(8,128)(2,1)} %get-tuple-element.25) | copy-start | bytes 1572868
  143.0 1.2 copy-start

commit v2 on v1

v2 whole, which is shorter than its diff:
```python
import math

import jax
import jax.numpy as jnp
from jax import lax
from jax.experimental import pallas as pl
from jax.experimental.pallas import tpu as pltpu
from jax.sharding import PartitionSpec as P

DH = 128
BLK = 128
NEG = -1e30
FACTOR = 1.0 / math.sqrt(DH)
F32 = jnp.float32
BF16 = jnp.bfloat16
HD = 4
MOST = 5
ROWS = MOST * BLK
KEYS = ROWS + 16
SEQ = 256
CAP = (6, 4)
CHUNKS = ((0, 256), (256, 512), (512, 640))


def kernel(
    q_in, g_in, k_in, v_in, meta_in, hdr_in, hidx,
    q_out, k_out, v_out, h_out,
    wk, sbuf, land, imp, cqg, ckv, probs, mixes, bias, gr, rsend, rland, rw, ost, back,
    meta, meta_s, padw, tabf, table, hb, hd, hz, hx, hs, ry,
    e_send, e_recv, own_sem, f_send, f_recv, r_send, r_recv, x_send, x_recv, xown_sem,
    m_send, m_recv, ms_sem, hs_send, hs_recv, ht_send, ht_recv,
):
    e = lax.axis_index("seq")
    h = lax.axis_index("head")
    core = lax.rem(e, 2)
    chip = e // 2
    j8 = lax.rem(e, 8)
    x4 = lax.rem(e // 8, 4)
    z8 = e // 32

    def wrap(index):
        return lax.rem(index + SEQ, SEQ)

    step = 2 * core - 1
    peer = e + 1 - 2 * core
    sends_to = (wrap(e + 2 * step), wrap(e - 2 * step))
    comes_from = (sends_to[1], sends_to[0])
    left, right = wrap(2 * chip - 2), wrap(2 * chip + 2)

    def y_peer(d):
        return e - j8 + lax.rem(j8 + d, 8)

    def x_peer(d):
        return e - 8 * x4 + 8 * lax.rem(x4 + d, 4)

    def z_peer(d):
        return e - 32 * z8 + 32 * lax.rem(z8 + d, 8)

    barrier = pltpu.get_barrier_semaphore()

    def greet(device, other):
        pl.semaphore_signal(barrier, inc=1, device_id=(device, other), device_id_type=pl.DeviceIdType.MESH)

    for d in range(1, 8):
        greet(y_peer(d), h)
        greet(z_peer(d), h)
    for d in range(1, 4):
        greet(x_peer(d), h)
    for c in range(2):
        greet(left + c, h)
        greet(right + c, h)
    greet(e, 1 - h)
    greet(peer, 1 - h)

    def remote(src, dst, send, recv, device, other):
        return pltpu.make_async_remote_copy(
            src_ref=src, dst_ref=dst, send_sem=send, recv_sem=recv,
            device_id=(device, other), device_id_type=pl.DeviceIdType.MESH,
        )

    ins = (q_in, g_in, k_in, v_in)

    def own_copy(array, head):
        cols = pl.ds(pl.multiple_of((core * HD + head) * DH, DH), DH)
        there = wk.at[head, array, pl.ds(2 * core, 2)]
        return pltpu.make_async_copy(ins[array].at[:, :, cols], there, own_sem.at[head, array])

    def peer_copy(array, head):
        cols = pl.ds(pl.multiple_of(((1 - core) * HD + head) * DH, DH), DH)
        there = wk.at[head, array, pl.ds(2 * core, 2)]
        return remote(ins[array].at[:, :, cols], there, e_send.at[head, array], e_recv.at[head, array], peer, h)

    tabf[pl.ds(j8, 1)] = hdr_in[...][None]
    meta[pl.ds(2 + core, 1)] = meta_in[...][None]
    for array in range(4):
        for head in range(HD):
            own_copy(array, head).start()

    pl.semaphore_wait(barrier, 23)

    meta_to = ((peer, 2 + core), (left, 4 + core), (left + 1, 4 + core), (right, core), (right + 1, core))

    def meta_copy(kind):
        device, slot = meta_to[kind]
        return remote(meta.at[2 + core], meta.at[slot], m_send.at[kind], m_recv.at[slot], device, h)

    def meta_arrival(slot):
        return remote(meta.at[2 + core], meta.at[slot], m_send.at[0], m_recv.at[slot], peer, h)

    for kind in range(5):
        meta_copy(kind).start()

    def row_y(d):
        return remote(tabf.at[j8], tabf.at[j8], hs_send.at[d - 1], hs_recv.at[d - 1], y_peer(d), h)

    def row_x(d):
        part = table.at[pl.ds(4 * (4 * z8 + x4), 4)]
        return remote(part, part, hs_send.at[6 + d], hs_recv.at[6 + d], x_peer(d), h)

    def row_z(d):
        part = table.at[pl.ds(16 * z8, 16)]
        return remote(part, part, hs_send.at[9 + d], hs_recv.at[9 + d], z_peer(d), h)

    for d in range(1, 8):
        row_y(d).start()
    for array in range(4):
        for head in range(HD):
            peer_copy(array, head).start()

    for slot in (0, 1, 4, 5):
        meta_arrival(slot).wait_recv()
    meta_arrival(3 - core).wait_recv()
    to_scalar = pltpu.make_async_copy(meta, meta_s, ms_sem)
    to_scalar.start()
    to_scalar.wait()
    start_x, size_x, id_x = meta_s[2, 2, 0] - 4 * chip, meta_s[2, 4, 0], meta_s[2, 6, 0]
    start_y, size_y, id_y = meta_s[3, 3, 0] - 4 * chip, meta_s[3, 5, 0], meta_s[3, 7, 0]
    a_x = jnp.maximum(-start_x, 0)
    b_x = size_x - a_x
    b_y = jnp.maximum(start_y + size_y - 4, 0)
    a_y = size_y - b_y
    cross_x, cross_y = a_x > 0, b_y > 0
    same = id_x == id_y
    on_x = jnp.logical_not(same & cross_y)
    on_y = jnp.logical_not(same) | cross_y

    def left_heads(a, b):
        return jnp.where(b == 1, 3, jnp.where(a == 1, 1, jnp.where(b == 2, 3 - core, 2 - core)))

    split_x, split_y = left_heads(a_x, b_x), left_heads(a_y, b_y)

    def home_x(head):
        return jnp.logical_not(cross_x) | (head >= split_x)

    def home_y(head):
        return jnp.logical_not(cross_y) | (head < split_y)

    is_x = (core == 1, core == 0)

    def pick(unit, of_x, of_y):
        return jnp.where(is_x[unit], of_x, of_y)

    start_u = [pick(u, start_x, start_y) for u in range(2)]
    size_u = [pick(u, size_x, size_y) for u in range(2)]
    width_u = [pick(u, a_x, b_y) for u in range(2)]
    given_u = [pick(u, b_x, a_y) for u in range(2)]
    id_u = [pick(u, id_x, id_y) for u in range(2)]
    on_u = [pick(u, on_x, on_y) for u in range(2)]

    def over(slot, width):
        by = [slot // n for n in range(1, 5)]
        return jnp.where(width == 2, by[1], jnp.where(width == 3, by[2], jnp.where(width == 4, by[3], by[0])))

    def rest(slot, width):
        return slot - over(slot, width) * jnp.clip(width, 1, 4)

    for d in range(1, 8):
        row_y(d).wait_recv()
    rows = tabf[...].astype(F32)
    halves = [
        jnp.concatenate([rows[:, HD * c : HD * c + HD], rows[:, 8 + HD * c : 8 + HD * c + HD]], axis=1)
        for c in range(2)
    ]
    rows = jnp.where(core == 0, halves[0], halves[1])
    table[pl.ds(4 * (4 * z8 + x4), 4)] = rows.reshape(4, 16, DH).astype(BF16)
    for d in range(1, 4):
        row_x(d).start()

    for array in range(4):
        for head in range(HD):
            own_copy(array, head).wait()
            peer_copy(array, head).wait_recv()

    def forward(d, slot):
        at = 6 * d + slot
        return remote(sbuf.at[at], land.at[at], f_send.at[at], f_recv.at[at], sends_to[d], h)

    def send(d, slot):
        unit = 1 - d
        width = given_u[unit]
        order = jnp.clip(over(slot, width), 0, HD - 1)
        part = rest(slot, width)
        head = pick(unit, order, HD - 1 - order)
        block = jnp.clip(pick(unit, part, 4 - a_y + part), 0, 3)
        sbuf[6 * d + slot] = wk[head, :, block]
        forward(d, slot).start()

    for slot in range(4):
        for d in range(2):
            send(d, slot)
    for d in range(1, 4):
        row_x(d).wait_recv()
    for d in range(1, 8):
        row_z(d).start()
    for slot in range(4, 6):
        send(0, slot)

    for slot in range(6):
        for block in range(2):
            padw[2 * slot + block] = jnp.broadcast_to(meta[slot, block : block + 1, :].astype(F32), (8, BLK))
    for u in range(2):
        for p in range(MOST):
            line = padw[jnp.clip(start_u[u] + p + 4, 0, 11)][0:1]
            full = jnp.broadcast_to(line, (BLK, BLK)).T
            full = jnp.where(p < size_u[u], full, 0.0)
            bias[u, p * BLK : p * BLK + BLK, :] = jnp.where(full > 0.0, 0.0, NEG)
        at = lax.broadcasted_iota(jnp.int32, (16, BLK), 0)
        bias[u, ROWS:KEYS, :] = jnp.where(at < 2, 0.0, NEG)

    for d in range(1, 8):
        row_z(d).wait_recv()
    names = []
    for u in range(2):
        for slot in range(2):
            row = hidx[2 * id_u[u] + slot]
            pair = table[lax.div(row, 2)].astype(F32)
            hb[2 * u + slot] = jnp.where(lax.rem(row, 2) == 0, pair[0:8], pair[8:16])
            names.append(jnp.where(on_u[u], row, -1))

    def nt(a, b):
        return lax.dot_general(a, b, (((1,), (1,)), ((), ())), preferred_element_type=F32)

    def give_back(d, slot):
        at = 6 * d + slot
        return remote(rsend.at[at], rland.at[at], r_send.at[at], r_recv.at[at], comes_from[d], h)

    def send_back(d, slot):
        part = rest(slot, width_u[d])
        turn = jnp.clip(over(slot, width_u[d]), 0, HD - 1)
        p = jnp.clip(pick(d, part, part + 4 - start_u[d]), 0, MOST - 1)
        rsend[6 * d + slot] = gr[d, turn, :, p]
        give_back(d, slot).start()

    def work(turn, carry):
        @pl.when(turn == 0)
        def _():
            for slot in range(4):
                for d in range(2):
                    forward(d, slot).wait_recv()
                    imp[6 * d + slot] = land[6 * d + slot]

        @pl.when(turn == 1)
        def _():
            for slot in range(4, 6):
                forward(0, slot).wait_recv()
                imp[slot] = land[slot]

        for u in range(2):
            head = turn + (core if u == 0 else 1 - core) * (HD - 1 - 2 * turn)
            last = jnp.where(turn == 0, 3, CAP[u] - 1)
            for p in range(MOST):
                there = start_u[u] + p
                slot = turn * width_u[u] + pick(u, p, there - 4)
                outside = (there < 0) | (there > 3)
                far = imp[6 * u + jnp.clip(slot, 0, last)]
                near = wk[head, :, jnp.clip(there, 0, 3)]
                rows = jnp.where(outside, far, near)
                span = slice(p * BLK, p * BLK + BLK)
                cqg[u, :, span, :] = jnp.where(p < size_u[u], rows[0:2], jnp.zeros_like(rows[0:2]))
                ckv[u, :, span, :] = rows[2:4]
            for array in range(2):
                at = pl.ds(array * HD + head, 1)
                lines = [hb[2 * u + slot, at, :] for slot in range(2)] + [jnp.zeros((14, DH), F32)]
                ckv[u, array, ROWS:KEYS, :] = jnp.concatenate(lines, axis=0).astype(BF16)
            for lo, hi in CHUNKS:
                q = cqg[u, 0, lo:hi, :]
                g = cqg[u, 1, lo:hi, :]
                keys = ckv[u, 0]
                values = ckv[u, 1]
                mask = bias[u]
                if hi - lo == 256:
                    mask = jnp.concatenate([mask, mask], axis=1)
                score = nt(keys, q) * FACTOR + mask
                top = jnp.max(score, axis=0, keepdims=True)
                grown = jnp.exp(score - top)
                prob = grown * (1.0 / jnp.sum(grown, axis=0, keepdims=True))
                low = prob.astype(BF16)
                dprob = nt(values, g)
                delta = jnp.sum(low.astype(F32) * dprob, axis=0, keepdims=True)
                mixing = (FACTOR * prob * (dprob - delta)).astype(BF16)
                probs[u, :, lo:hi] = low
                mixes[u, :, lo:hi] = mixing
                q_grad = lax.dot_general(mixing, keys, (((0,), (0,)), ((), ())), preferred_element_type=F32)
                gr[u, turn, 0, lo // BLK : hi // BLK] = q_grad.astype(BF16).reshape(-1, BLK, DH)
            here = pick(u, home_x(head), home_y(head))
            for array, weights in ((0, mixes), (1, probs)):
                total = jnp.dot(weights[u], cqg[u, array], preferred_element_type=F32)
                gr[u, turn, 1 + array] = total[0:ROWS].astype(BF16).reshape(MOST, BLK, DH)
                for slot in range(2):
                    line = total[ROWS + slot : ROWS + slot + 1]
                    hd[2 * u + slot, pl.ds(array * HD + head, 1), :] = jnp.where(here, line, 0.0)

        for ready, slots in ((0, (0,)), (1, (1, 3)), (2, (2, 4, 5))):

            @pl.when(turn == ready)
            def _(slots=slots):
                for slot in slots:
                    for d in range(2):
                        if slot < CAP[d]:
                            send_back(d, slot)

        return carry

    lax.fori_loop(0, HD, work, 0)

    tags = [jnp.full((1, DH), name).astype(F32) for name in names] + [jnp.full((12, DH), -1.0, F32)]
    block = jnp.concatenate([hd[slot] for slot in range(4)] + tags, axis=0)
    hz[pl.ds(z8, 1)] = block.astype(BF16)[None]

    def out_z(d):
        return remote(hz.at[z8], hz.at[z8], ht_send.at[d - 1], ht_recv.at[d - 1], z_peer(d), h)

    def out_x(d):
        return remote(hx.at[x4], hx.at[x4], ht_send.at[6 + d], ht_recv.at[6 + d], x_peer(d), h)

    def out_y(d):
        src = hs.at[lax.rem(j8 + d, 8)]
        return remote(src, ry.at[j8], ht_send.at[9 + d], ht_recv.at[9 + d], y_peer(d), h)

    for d in range(1, 8):
        out_z(d).start()

    mine = 2 * core + h

    def column(head):
        return pl.ds(pl.multiple_of(h * 1024 + (core * HD + head) * DH, DH), DH)

    def deliver(d, head):
        there = lax.rem(mine + d, 4)
        return remote(
            ost.at[head, there], back.at[:, :, column(head)], x_send.at[head, d - 1], x_recv.at[head, d - 1],
            2 * chip + there // 2, lax.rem(there, 2),
        )

    def keep(head):
        return pltpu.make_async_copy(ost.at[head, mine], back.at[:, :, column(head)], xown_sem.at[head])

    for d in range(2):
        for slot in range(CAP[d]):
            give_back(d, slot).wait_recv()
            rw[6 * d + slot] = rland[6 * d + slot]
    unit_x = jnp.where(core == 1, 0, 1)

    def assemble(head, carry):
        for j in range(4):
            in_x = on_x & (j < start_x + size_x)
            unit = jnp.where(in_x, unit_x, 1 - unit_x)
            turn = jnp.where(in_x, HD - 1 - head, head)
            p = jnp.clip(jnp.where(in_x, j - start_x, j - start_y), 0, MOST - 1)
            slot = jnp.where(in_x, head * b_x + j, (HD - 1 - head) * a_y + j - start_y)
            here = jnp.where(in_x, home_x(head).astype(jnp.int32), home_y(head).astype(jnp.int32)) > 0
            most = jnp.where(unit == 1, CAP[0] - 1, CAP[1] - 1)
            at = 6 * (1 - unit) + jnp.clip(slot, 0, most)
            worked = gr[unit, turn, :, p]
            ost[head, j] = jnp.where(here, worked, rw[at])
        for d in range(1, 4):
            deliver(d, head).start()
        keep(head).start()
        return carry

    lax.fori_loop(0, HD, assemble, 0)

    for d in range(1, 8):
        out_z(d).wait_recv()
    hx[pl.ds(x4, 1)] = hz[...].reshape(1, 8 * 48, DH)
    for d in range(1, 4):
        out_x(d).start()
    for d in range(1, 4):
        out_x(d).wait_recv()
    first = 32 * z8 + 8 * x4

    def gather(at, totals):
        block = hx[at // 8, pl.ds(pl.multiple_of(lax.rem(at, 8) * 48, 16), 48), :].astype(F32)
        totals = list(totals)
        for slot in range(4):
            tag = jnp.broadcast_to(block[32 + slot : 33 + slot], (8, DH)) - first.astype(F32)
            for j in range(8):
                totals[j] = totals[j] + jnp.where(tag == float(j), block[8 * slot : 8 * slot + 8], 0.0)
        return tuple(totals)

    totals = lax.fori_loop(0, 32, gather, tuple(jnp.zeros((8, DH), F32) for _ in range(8)))
    for j in range(8):
        hs[j] = totals[j]
    for d in range(1, 8):
        out_y(d).start()
    ry[pl.ds(j8, 1)] = hs[pl.ds(j8, 1)]
    for d in range(1, 8):
        out_y(d).wait_recv()
    halves = [ry[c] + ry[c + 2] + ry[c + 4] + ry[c + 6] for c in range(2)]
    lines = [halves[0][0:4], halves[1][0:4], halves[0][4:8], halves[1][4:8]]
    h_out[...] = jnp.concatenate(lines, axis=0).astype(BF16)

    def settle(head, carry):
        for d in range(1, 4):
            deliver(d, head).wait_recv()
        keep(head).wait()
        return carry

    lax.fori_loop(0, HD, settle, 0)
    for array, out in ((0, q_out), (1, k_out), (2, v_out)):
        out[...] = back[array]

    for array in range(4):
        for head in range(HD):
            peer_copy(array, head).wait_send()
    for d in range(2):
        for slot in range(CAP[d]):
            forward(d, slot).wait_send()
            give_back(d, slot).wait_send()
    for head in range(HD):
        for d in range(1, 4):
            deliver(d, head).wait_send()
    for kind in range(5):
        meta_copy(kind).wait_send()
    for d in range(1, 8):
        row_y(d).wait_send()
        row_z(d).wait_send()
        out_y(d).wait_send()
        out_z(d).wait_send()
    for d in range(1, 4):
        row_x(d).wait_send()
        out_x(d).wait_send()


def body(
    queries, key_rows, value_rows, out_grad, padding, header_keys, header_values,
    neighbours, slot_valid, crystal_ids, header_index,
):
    used = slot_valid > 0
    size = jnp.sum(used.astype(jnp.int32), axis=1)
    start = jnp.min(jnp.where(used, neighbours, 1 << 20), axis=1)
    wide = [jnp.broadcast_to(each[:, None], (2, BLK)) for each in (start, size, crystal_ids)]
    meta = jnp.concatenate([padding.reshape(2, BLK)] + wide)
    hdr = jnp.concatenate([header_keys.reshape(8, DH), header_values.reshape(8, DH)])
    grad = jax.ShapeDtypeStruct((BLK, 2048), BF16)
    vmem = pl.BlockSpec(memory_space=pltpu.VMEM)
    hbm = pl.BlockSpec(memory_space=pl.ANY)
    dma = pltpu.SemaphoreType.DMA
    q_grad, k_grad, v_grad, h_grad = pl.pallas_call(
        kernel,
        out_shape=(grad, grad, grad, jax.ShapeDtypeStruct((16, DH), BF16)),
        in_specs=[hbm] * 4 + [vmem] * 2 + [pl.BlockSpec(memory_space=pltpu.SMEM)],
        out_specs=[vmem] * 4,
        scratch_shapes=[
            pltpu.VMEM((HD, 4, 4, BLK, DH), BF16),
            pltpu.VMEM((10, 4, BLK, DH), BF16),
            pltpu.VMEM((10, 4, BLK, DH), BF16),
            pltpu.VMEM((10, 4, BLK, DH), BF16),
            pltpu.VMEM((2, 2, ROWS, DH), BF16),
            pltpu.VMEM((2, 2, KEYS, DH), BF16),
            pltpu.VMEM((2, KEYS, ROWS), BF16),
            pltpu.VMEM((2, KEYS, ROWS), BF16),
            pltpu.VMEM((2, KEYS, BLK), F32),
            pltpu.VMEM((2, HD, 3, MOST, BLK, DH), BF16),
            pltpu.VMEM((10, 3, BLK, DH), BF16),
            pltpu.VMEM((10, 3, BLK, DH), BF16),
            pltpu.VMEM((10, 3, BLK, DH), BF16),
            pltpu.VMEM((HD, 4, 3, BLK, DH), BF16),
            pltpu.VMEM((3, BLK, 2048), BF16),
            pltpu.VMEM((6, 8, BLK), jnp.int32),
            pltpu.SMEM((6, 8, BLK), jnp.int32),
            pltpu.VMEM((12, 8, BLK), F32),
            pltpu.VMEM((8, 16, DH), BF16),
            pltpu.VMEM((SEQ // 2, 16, DH), BF16),
            pltpu.VMEM((4, 8, DH), F32),
            pltpu.VMEM((4, 8, DH), F32),
            pltpu.VMEM((8, 48, DH), BF16),
            pltpu.VMEM((4, 8 * 48, DH), BF16),
            pltpu.VMEM((8, 8, DH), F32),
            pltpu.VMEM((8, 8, DH), F32),
            dma((HD, 4)),
            dma((HD, 4)),
            dma((HD, 4)),
            dma((10,)),
            dma((10,)),
            dma((10,)),
            dma((10,)),
            dma((HD, 3)),
            dma((HD, 3)),
            dma((HD,)),
            dma((5,)),
            dma((6,)),
            dma,
            dma((17,)),
            dma((17,)),
            dma((17,)),
            dma((17,)),
        ],
        compiler_params=pltpu.CompilerParams(
            collective_id=0, has_side_effects=True, vmem_limit_bytes=56 * 1024 * 1024
        ),
    )(*[each.reshape(2, BLK, 1024) for each in (queries, out_grad, key_rows, value_rows)], meta, hdr, header_index.reshape(-1))
    return (q_grad, k_grad, v_grad, h_grad[:8].reshape(1, 1024), h_grad[8:].reshape(1, 1024))


def solution(mesh):
    in_specs = (
        P("seq", "head"),
        P("seq", "head"),
        P("seq", "head"),
        P("seq", "head"),
        P("seq"),
        P("seq", "head"),
        P("seq", "head"),
        P("seq", None),
        P("seq", None),
        P("seq"),
        P(),
    )
    out_specs = (
        P(("seq", "head"), None),
        P(("seq", "head"), None),
        P(("seq", "head"), None),
        P("seq", "head"),
        P("seq", "head"),
    )
    return jax.shard_map(body, mesh=mesh, in_specs=in_specs, out_specs=out_specs, check_vma=False)
```

time: 146 us -> 116 us (0.79)
  the two profiles are of different devices: /device:TPU:7 before, /device:TPU:29 now
where the time goes in v2:
time: 116 us; the launch traced here: 115 us
  Pallas kernels  104 us (90%)
  local copies, waits for them, and re-layouts  8.89 us (8%)
  other arithmetic  1.45 us (1%)
    pallas_call x1, Pallas kernels, body(): pl.pallas_call(kernel, out_shape=(grad, grad, grad, jax.ShapeDtypeStruct(...  104 us
    unnamed x25, local copies, waits for them, and re-layouts  7.35 us

profile of v2, /device:TPU:29, one launch (start us, length us, event | category | flops | bytes accessed | tf_op | source)
XLA Modules:
  0.0 115.4 jit_solution(9003832213455803650)
XLA Ops:
  0.6 0.0 copy-start.9
  0.6 0.0 copy-start.7
  0.7 0.6 copy-done.9
  1.3 0.1 pad.5.clone
  1.4 0.0 copy-done.7
  1.4 0.6 copy-done.6
  2.0 0.1 select_reduce_fusion
  2.1 0.1 pad.4.clone
  2.2 0.1 pad.3.clone
  2.3 0.6 copy-done.8
  2.9 0.7 add_add_fusion.meta_in
  3.5 0.0 copy-done.3
  3.6 0.7 copy-done.4
  4.3 0.6 pad_maximum_fusion.hdr_in
  4.9 0.1 copy-done.5
  4.9 0.1 copy.16
  5.1 0.7 reshape.50.hidx
  5.8 104.4 %shard_map.146 = (bf16[128,2048]{1,0:T(8,128)(2,1)}, bf16[128,2048]{1,0:T(8,128)(2,1)}, bf16[128,2048]{1,0:T(8,128)(2,1)}, bf16[16,128]{1,0:T(8,128)(2,1)}) custom-call(bf16[2,128,1024]{2,1,0:T(8,128)(2,1)} %bitcast.17, bf16[2,128,1024]{2,1,0:T(8,128)(2,1)} %bitcast.18, bf16[2,128,1024]{2,1,0:T(8,128)(2,1)} %bitcast.19, bf16[2,128,1024]{2,1,0:T(8,128)(2,1)} %bitcast.20, ...), custom_call_target="tpu_custom_call" | custom-call | tf_op jit(solution)/shard_map/pallas_call | solution.py:459
  110.2 0.7 copy-done.2
  110.8 0.6 copy_bitcast_fusion
  111.4 1.9 %copy.24 = bf16[128,2048]{1,0:T(8,128)(2,1)} copy(bf16[128,2048]{1,0:T(8,128)(2,1)} %get-tuple-element.24) | data formatting | bytes 1048576
  113.4 0.8 copy.25
  114.2 0.4 copy-done
  114.6 0.8 copy.26
  (12 shorter events, 0.1 us)
Async XLA Ops:
  0.6 0.7 copy-start.9
  0.6 0.7 copy-start.7
  1.3 0.7 copy-start.6
  2.2 0.7 copy-start.8
  2.2 1.4 %copy-start.3 = (bf16[1,1024]{1,0:T(2,128)(2,1)S(1)}, bf16[1,1024]{1,0:T(2,128)(2,1)}, u32[]{:S(2)}) copy-start(bf16[1,1024]{1,0:T(2,128)(2,1)} %param.17) | copy-start | bytes 6148
  3.5 0.7 copy-start.4
  4.3 0.7 copy-start.5
  110.1 0.7 copy-start.2
  111.4 1.9 %copy-start.1 = (bf16[128,2048]{1,0:T(8,128)(2,1)S(1)}, bf16[128,2048]{1,0:T(8,128)(2,1)}, u32[]{:S(2)}) copy-start(bf16[128,2048]{1,0:T(8,128)(2,1)} %get-tuple-element.25) | copy-start | bytes 1572868
  113.4 1.2 %copy-start = (bf16[128,2048]{1,0:T(8,128)(2,1)S(1)}, bf16[128,2048]{1,0:T(8,128)(2,1)}, u32[]{:S(2)}) copy-start(bf16[128,2048]{1,0:T(8,128)(2,1)} %get-tuple-element.26) | copy-start | bytes 1572868

commit v3 on v2

--- a/solution.py
+++ b/solution.py
@@ -23,7 +23,7 @@
 
 
 def kernel(
-    q_in, g_in, k_in, v_in, meta_in, hdr_in, hidx,
+    q_in, g_in, k_in, v_in, pad_in, hk_in, hv_in, lists, valid, ids, hidx,
     q_out, k_out, v_out, h_out,
     wk, sbuf, land, imp, cqg, ckv, probs, mixes, bias, gr, rsend, rland, rw, ost, back,
     meta, meta_s, padw, tabf, table, hb, hd, hz, hx, hs, ry,
@@ -90,11 +90,22 @@
         there = wk.at[head, array, pl.ds(2 * core, 2)]
         return remote(ins[array].at[:, :, cols], there, e_send.at[head, array], e_recv.at[head, array], peer, h)
 
-    tabf[pl.ds(j8, 1)] = hdr_in[...][None]
-    meta[pl.ds(2 + core, 1)] = meta_in[...][None]
     for array in range(4):
         for head in range(HD):
             own_copy(array, head).start()
+    lines = [each[:, DH * i : DH * i + DH] for each in (hk_in, hv_in) for i in range(8)]
+    tabf[pl.ds(j8, 1)] = jnp.concatenate([line.astype(F32) for line in lines], axis=0).astype(BF16)[None]
+    starts, sizes = [], []
+    for block in range(2):
+        first, size = jnp.int32(1 << 20), jnp.int32(0)
+        for slot in range(MOST):
+            used = valid[block, slot] > 0
+            first = jnp.where(used, jnp.minimum(first, lists[block, slot]), first)
+            size = size + jnp.where(used, 1, 0)
+        starts.append(first)
+        sizes.append(size)
+    lines = [jnp.full((1, BLK), each, jnp.int32) for each in starts + sizes + [ids[0], ids[1]]]
+    meta[pl.ds(2 + core, 1)] = jnp.concatenate([pad_in[...]] + lines, axis=0)[None]
 
     pl.semaphore_wait(barrier, 23)
 
@@ -107,8 +118,6 @@
     def meta_arrival(slot):
         return remote(meta.at[2 + core], meta.at[slot], m_send.at[0], m_recv.at[slot], peer, h)
 
-    for kind in range(5):
-        meta_copy(kind).start()
 
     def row_y(d):
         return remote(tabf.at[j8], tabf.at[j8], hs_send.at[d - 1], hs_recv.at[d - 1], y_peer(d), h)
@@ -123,15 +132,33 @@
 
     for d in range(1, 8):
         row_y(d).start()
+    for kind in range(5):
+        meta_copy(kind).start()
     for array in range(4):
         for head in range(HD):
             peer_copy(array, head).start()
+
+    for d in range(1, 8):
+        row_y(d).wait_recv()
+    rows = tabf[...].astype(F32)
+    halves = [
+        jnp.concatenate([rows[:, HD * c : HD * c + HD], rows[:, 8 + HD * c : 8 + HD * c + HD]], axis=1)
+        for c in range(2)
+    ]
+    rows = jnp.where(core == 0, halves[0], halves[1])
+    table[pl.ds(4 * (4 * z8 + x4), 4)] = rows.reshape(4, 16, DH).astype(BF16)
+    for d in range(1, 4):
+        row_x(d).start()
 
     for slot in (0, 1, 4, 5):
         meta_arrival(slot).wait_recv()
     meta_arrival(3 - core).wait_recv()
     to_scalar = pltpu.make_async_copy(meta, meta_s, ms_sem)
     to_scalar.start()
+    for d in range(1, 4):
+        row_x(d).wait_recv()
+    for d in range(1, 8):
+        row_z(d).start()
     to_scalar.wait()
     start_x, size_x, id_x = meta_s[2, 2, 0] - 4 * chip, meta_s[2, 4, 0], meta_s[2, 6, 0]
     start_y, size_y, id_y = meta_s[3, 3, 0] - 4 * chip, meta_s[3, 5, 0], meta_s[3, 7, 0]
@@ -174,18 +201,6 @@
     def rest(slot, width):
         return slot - over(slot, width) * jnp.clip(width, 1, 4)
 
-    for d in range(1, 8):
-        row_y(d).wait_recv()
-    rows = tabf[...].astype(F32)
-    halves = [
-        jnp.concatenate([rows[:, HD * c : HD * c + HD], rows[:, 8 + HD * c : 8 + HD * c + HD]], axis=1)
-        for c in range(2)
-    ]
-    rows = jnp.where(core == 0, halves[0], halves[1])
-    table[pl.ds(4 * (4 * z8 + x4), 4)] = rows.reshape(4, 16, DH).astype(BF16)
-    for d in range(1, 4):
-        row_x(d).start()
-
     for array in range(4):
         for head in range(HD):
             own_copy(array, head).wait()
@@ -208,10 +223,6 @@
     for slot in range(4):
         for d in range(2):
             send(d, slot)
-    for d in range(1, 4):
-        row_x(d).wait_recv()
-    for d in range(1, 8):
-        row_z(d).start()
     for slot in range(4, 6):
         send(0, slot)
 
@@ -232,7 +243,7 @@
     names = []
     for u in range(2):
         for slot in range(2):
-            row = hidx[2 * id_u[u] + slot]
+            row = hidx[slot, id_u[u]]
             pair = table[lax.div(row, 2)].astype(F32)
             hb[2 * u + slot] = jnp.where(lax.rem(row, 2) == 0, pair[0:8], pair[8:16])
             names.append(jnp.where(on_u[u], row, -1))
@@ -355,8 +366,8 @@
     def keep(head):
         return pltpu.make_async_copy(ost.at[head, mine], back.at[:, :, column(head)], xown_sem.at[head])
 
-    for d in range(2):
-        for slot in range(CAP[d]):
+    for slot in range(4):
+        for d in range(2):
             give_back(d, slot).wait_recv()
             rw[6 * d + slot] = rland[6 * d + slot]
     unit_x = jnp.where(core == 1, 0, 1)
@@ -365,20 +376,27 @@
         for j in range(4):
             in_x = on_x & (j < start_x + size_x)
             unit = jnp.where(in_x, unit_x, 1 - unit_x)
-            turn = jnp.where(in_x, HD - 1 - head, head)
+            when = jnp.where(in_x, HD - 1 - head, head)
             p = jnp.clip(jnp.where(in_x, j - start_x, j - start_y), 0, MOST - 1)
             slot = jnp.where(in_x, head * b_x + j, (HD - 1 - head) * a_y + j - start_y)
             here = jnp.where(in_x, home_x(head).astype(jnp.int32), home_y(head).astype(jnp.int32)) > 0
             most = jnp.where(unit == 1, CAP[0] - 1, CAP[1] - 1)
             at = 6 * (1 - unit) + jnp.clip(slot, 0, most)
-            worked = gr[unit, turn, :, p]
+            worked = gr[unit, when, :, p]
             ost[head, j] = jnp.where(here, worked, rw[at])
         for d in range(1, 4):
             deliver(d, head).start()
         keep(head).start()
         return carry
 
-    lax.fori_loop(0, HD, assemble, 0)
+    def assemble_pair(one, two):
+        lax.fori_loop(0, 2, lambda i, carry: assemble(one + (two - one) * i, carry), 0)
+
+    assemble_pair(0, 3)
+    for slot in range(4, 6):
+        give_back(0, slot).wait_recv()
+        rw[slot] = rland[slot]
+    assemble_pair(1, 2)
 
     for d in range(1, 8):
         out_z(d).wait_recv()
@@ -442,16 +460,20 @@
         out_x(d).wait_send()
 
 
+def finish(q_in, k_in, v_in, h_in, q_out, k_out, v_out, hk_out, hv_out):
+    q_out[...] = q_in[...]
+    k_out[...] = k_in[...]
+    v_out[...] = v_in[...]
+    rows = h_in[...].astype(F32)
+    for i in range(8):
+        hk_out[:, DH * i : DH * i + DH] = rows[i : i + 1].astype(BF16)
+        hv_out[:, DH * i : DH * i + DH] = rows[8 + i : 9 + i].astype(BF16)
+
+
 def body(
     queries, key_rows, value_rows, out_grad, padding, header_keys, header_values,
     neighbours, slot_valid, crystal_ids, header_index,
 ):
-    used = slot_valid > 0
-    size = jnp.sum(used.astype(jnp.int32), axis=1)
-    start = jnp.min(jnp.where(used, neighbours, 1 << 20), axis=1)
-    wide = [jnp.broadcast_to(each[:, None], (2, BLK)) for each in (start, size, crystal_ids)]
-    meta = jnp.concatenate([padding.reshape(2, BLK)] + wide)
-    hdr = jnp.concatenate([header_keys.reshape(8, DH), header_values.reshape(8, DH)])
     grad = jax.ShapeDtypeStruct((BLK, 2048), BF16)
     vmem = pl.BlockSpec(memory_space=pltpu.VMEM)
     hbm = pl.BlockSpec(memory_space=pl.ANY)
@@ -459,7 +481,7 @@
     q_grad, k_grad, v_grad, h_grad = pl.pallas_call(
         kernel,
         out_shape=(grad, grad, grad, jax.ShapeDtypeStruct((16, DH), BF16)),
-        in_specs=[hbm] * 4 + [vmem] * 2 + [pl.BlockSpec(memory_space=pltpu.SMEM)],
+        in_specs=[hbm] * 4 + [vmem] * 3 + [pl.BlockSpec(memory_space=pltpu.SMEM)] * 4,
         out_specs=[vmem] * 4,
         scratch_shapes=[
             pltpu.VMEM((HD, 4, 4, BLK, DH), BF16),
@@ -509,8 +531,14 @@
         compiler_params=pltpu.CompilerParams(
             collective_id=0, has_side_effects=True, vmem_limit_bytes=56 * 1024 * 1024
         ),
-    )(*[each.reshape(2, BLK, 1024) for each in (queries, out_grad, key_rows, value_rows)], meta, hdr, header_index.reshape(-1))
-    return (q_grad, k_grad, v_grad, h_grad[:8].reshape(1, 1024), h_grad[8:].reshape(1, 1024))
+    )(*[each.reshape(2, BLK, 1024) for each in (queries, out_grad, key_rows, value_rows)], padding.reshape(2, BLK), header_keys, header_values,
+      neighbours, slot_valid, crystal_ids, header_index.T)
+    line = jax.ShapeDtypeStruct((1, 1024), BF16)
+    return pl.pallas_call(
+        finish,
+        out_shape=(grad, grad, grad, line, line),
+        compiler_params=pltpu.CompilerParams(vmem_limit_bytes=56 * 1024 * 1024),
+    )(q_grad, k_grad, v_grad, h_grad)
 
 
 def solution(mesh):

time: 116 us -> 106 us (0.914)
  the two profiles are of different devices: /device:TPU:29 before, /device:TPU:7 now
where the time goes in v3:
time: 106 us
  Pallas kernels  105 us (99%)
    pallas_call x1, Pallas kernels, body(): pl.pallas_call(kernel, out_shape=(grad, grad, grad, jax.ShapeDtypeStruct(...  103 us
    pallas_call x1, Pallas kernels, body(): pl.pallas_call(finish, out_shape=(grad, grad, grad, line, line), compiler...  2.54 us

profile of v3, /device:TPU:7, one launch (start us, length us, event | category | flops | bytes accessed | tf_op | source)
XLA Modules:
  0.0 105.7 jit_solution(7785836279216610585)
XLA Ops:
  0.6 102.6 %shard_map.146 = (bf16[128,2048]{1,0:T(8,128)(2,1)}, bf16[128,2048]{1,0:T(8,128)(2,1)}, bf16[128,2048]{1,0:T(8,128)(2,1)}, bf16[16,128]{1,0:T(8,128)(2,1)}) custom-call(bf16[2,128,1024]{2,1,0:T(8,128)(2,1)} %bitcast.6, bf16[2,128,1024]{2,1,0:T(8,128)(2,1)} %bitcast.7, bf16[2,128,1024]{2,1,0:T(8,128)(2,1)} %bitcast.8, bf16[2,128,1024]{2,1,0:T(8,128)(2,1)} %bitcast.9, ...), custom_call_target="tpu_custom_call" | custom-call | tf_op jit(solution)/shard_map/pallas_call | solution.py:481
  103.2 2.5 %shard_map.147 = (bf16[128,2048]{1,0:T(8,128)(2,1)}, bf16[128,2048]{1,0:T(8,128)(2,1)}, bf16[128,2048]{1,0:T(8,128)(2,1)}, bf16[1,1024]{1,0:T(2,128)(2,1)}, bf16[1,1024]{1,0:T(2,128)(2,1)}) custom-call(bf16[128,2048]{1,0:T(8,128)(2,1)} %get-tuple-element.9.q_in, bf16[128,2048]{1,0:T(8,128)(2,1)} %get-tuple-element.10.k_in, ...), custom_call_target="tpu_custom_call" | custom-call | tf_op jit(solution)/shard_map/pallas_call | solution.py:537

commit v4 on v3

--- a/solution.py
+++ b/solution.py
@@ -19,7 +19,7 @@
 KEYS = ROWS + 16
 SEQ = 256
 CAP = (6, 4)
-CHUNKS = ((0, 256), (256, 512), (512, 640))
+CHUNKS = ((0, 384), (384, 640))
 
 
 def kernel(
@@ -28,7 +28,7 @@
     wk, sbuf, land, imp, cqg, ckv, probs, mixes, bias, gr, rsend, rland, rw, ost, back,
     meta, meta_s, padw, tabf, table, hb, hd, hz, hx, hs, ry,
     e_send, e_recv, own_sem, f_send, f_recv, r_send, r_recv, x_send, x_recv, xown_sem,
-    m_send, m_recv, ms_sem, hs_send, hs_recv, ht_send, ht_recv,
+    edge_send, edge_recv, m_send, m_recv, ms_sem, hs_send, hs_recv, ht_send, ht_recv,
 ):
     e = lax.axis_index("seq")
     h = lax.axis_index("head")
@@ -109,6 +109,11 @@
 
     pl.semaphore_wait(barrier, 23)
 
+    def edge_copy(array):
+        cols = pl.ds(pl.multiple_of((core * HD + core * (HD - 1)) * DH, DH), DH)
+        src = ins[array].at[core, :, cols]
+        return remote(src, land.at[0, array], edge_send.at[array], edge_recv.at[array], sends_to[0], h)
+
     meta_to = ((peer, 2 + core), (left, 4 + core), (left + 1, 4 + core), (right, core), (right + 1, core))
 
     def meta_copy(kind):
@@ -135,9 +140,16 @@
     for kind in range(5):
         meta_copy(kind).start()
     for array in range(4):
+        edge_copy(array).start()
+    for array in range(4):
         for head in range(HD):
             peer_copy(array, head).start()
 
+    for slot in (0, 1, 4, 5):
+        meta_arrival(slot).wait_recv()
+    meta_arrival(3 - core).wait_recv()
+    to_scalar = pltpu.make_async_copy(meta, meta_s, ms_sem)
+    to_scalar.start()
     for d in range(1, 8):
         row_y(d).wait_recv()
     rows = tabf[...].astype(F32)
@@ -149,12 +161,6 @@
     table[pl.ds(4 * (4 * z8 + x4), 4)] = rows.reshape(4, 16, DH).astype(BF16)
     for d in range(1, 4):
         row_x(d).start()
-
-    for slot in (0, 1, 4, 5):
-        meta_arrival(slot).wait_recv()
-    meta_arrival(3 - core).wait_recv()
-    to_scalar = pltpu.make_async_copy(meta, meta_s, ms_sem)
-    to_scalar.start()
     for d in range(1, 4):
         row_x(d).wait_recv()
     for d in range(1, 8):
@@ -216,15 +222,14 @@
         order = jnp.clip(over(slot, width), 0, HD - 1)
         part = rest(slot, width)
         head = pick(unit, order, HD - 1 - order)
-        block = jnp.clip(pick(unit, part, 4 - a_y + part), 0, 3)
+        block = jnp.clip(pick(unit, part, 3 - part), 0, 3)
         sbuf[6 * d + slot] = wk[head, :, block]
         forward(d, slot).start()
 
+    for slot in range(1, 6):
+        send(0, slot)
     for slot in range(4):
-        for d in range(2):
-            send(d, slot)
-    for slot in range(4, 6):
-        send(0, slot)
+        send(1, slot)
 
     for slot in range(6):
         for block in range(2):
@@ -258,81 +263,96 @@
     def send_back(d, slot):
         part = rest(slot, width_u[d])
         turn = jnp.clip(over(slot, width_u[d]), 0, HD - 1)
-        p = jnp.clip(pick(d, part, part + 4 - start_u[d]), 0, MOST - 1)
+        p = jnp.clip(pick(d, a_x - 1 - part, part + 4 - start_u[d]), 0, MOST - 1)
         rsend[6 * d + slot] = gr[d, turn, :, p]
         give_back(d, slot).start()
 
-    def work(turn, carry):
-        @pl.when(turn == 0)
+    def work(n, carry):
+        late = n // 6
+        u = (1 - late) * (n // 3) + late * (n - 6)
+        turn = (1 - late) * lax.rem(n, 3) + late * 3
+
+        @pl.when(n == 0)
         def _():
-            for slot in range(4):
-                for d in range(2):
-                    forward(d, slot).wait_recv()
-                    imp[6 * d + slot] = land[6 * d + slot]
-
-        @pl.when(turn == 1)
+            for array in range(4):
+                edge_copy(array).wait_recv()
+            imp[0] = land[0]
+            for slot in range(1, 4):
+                forward(0, slot).wait_recv()
+                imp[slot] = land[slot]
+
+        @pl.when(n == 1)
         def _():
             for slot in range(4, 6):
                 forward(0, slot).wait_recv()
                 imp[slot] = land[slot]
 
-        for u in range(2):
-            head = turn + (core if u == 0 else 1 - core) * (HD - 1 - 2 * turn)
-            last = jnp.where(turn == 0, 3, CAP[u] - 1)
-            for p in range(MOST):
-                there = start_u[u] + p
-                slot = turn * width_u[u] + pick(u, p, there - 4)
-                outside = (there < 0) | (there > 3)
-                far = imp[6 * u + jnp.clip(slot, 0, last)]
-                near = wk[head, :, jnp.clip(there, 0, 3)]
-                rows = jnp.where(outside, far, near)
-                span = slice(p * BLK, p * BLK + BLK)
-                cqg[u, :, span, :] = jnp.where(p < size_u[u], rows[0:2], jnp.zeros_like(rows[0:2]))
-                ckv[u, :, span, :] = rows[2:4]
-            for array in range(2):
-                at = pl.ds(array * HD + head, 1)
-                lines = [hb[2 * u + slot, at, :] for slot in range(2)] + [jnp.zeros((14, DH), F32)]
-                ckv[u, array, ROWS:KEYS, :] = jnp.concatenate(lines, axis=0).astype(BF16)
-            for lo, hi in CHUNKS:
-                q = cqg[u, 0, lo:hi, :]
-                g = cqg[u, 1, lo:hi, :]
-                keys = ckv[u, 0]
-                values = ckv[u, 1]
-                mask = bias[u]
-                if hi - lo == 256:
-                    mask = jnp.concatenate([mask, mask], axis=1)
-                score = nt(keys, q) * FACTOR + mask
-                top = jnp.max(score, axis=0, keepdims=True)
-                grown = jnp.exp(score - top)
-                prob = grown * (1.0 / jnp.sum(grown, axis=0, keepdims=True))
-                low = prob.astype(BF16)
-                dprob = nt(values, g)
-                delta = jnp.sum(low.astype(F32) * dprob, axis=0, keepdims=True)
-                mixing = (FACTOR * prob * (dprob - delta)).astype(BF16)
-                probs[u, :, lo:hi] = low
-                mixes[u, :, lo:hi] = mixing
-                q_grad = lax.dot_general(mixing, keys, (((0,), (0,)), ((), ())), preferred_element_type=F32)
-                gr[u, turn, 0, lo // BLK : hi // BLK] = q_grad.astype(BF16).reshape(-1, BLK, DH)
-            here = pick(u, home_x(head), home_y(head))
-            for array, weights in ((0, mixes), (1, probs)):
-                total = jnp.dot(weights[u], cqg[u, array], preferred_element_type=F32)
-                gr[u, turn, 1 + array] = total[0:ROWS].astype(BF16).reshape(MOST, BLK, DH)
-                for slot in range(2):
-                    line = total[ROWS + slot : ROWS + slot + 1]
-                    hd[2 * u + slot, pl.ds(array * HD + head, 1), :] = jnp.where(here, line, 0.0)
-
-        for ready, slots in ((0, (0,)), (1, (1, 3)), (2, (2, 4, 5))):
-
-            @pl.when(turn == ready)
-            def _(slots=slots):
-                for slot in slots:
-                    for d in range(2):
+        @pl.when(n == 3)
+        def _():
+            for slot in range(4):
+                forward(1, slot).wait_recv()
+                imp[6 + slot] = land[6 + slot]
+
+        wide = u == 0
+        start = jnp.where(wide, start_u[0], start_u[1])
+        size = jnp.where(wide, size_u[0], size_u[1])
+        width = jnp.where(wide, width_u[0], width_u[1])
+        first = core + u * (1 - 2 * core) == 1
+        head = turn + (core + u * (1 - 2 * core)) * (HD - 1 - 2 * turn)
+        last = jnp.where((n == 0) | (u == 1), 3, CAP[0] - 1)
+        for p in range(MOST):
+            there = start + p
+            slot = turn * width + jnp.where(first, -1 - there, there - 4)
+            outside = (there < 0) | (there > 3)
+            far = imp[6 * u + jnp.clip(slot, 0, last)]
+            near = wk[head, :, jnp.clip(there, 0, 3)]
+            rows = jnp.where(outside, far, near)
+            span = slice(p * BLK, p * BLK + BLK)
+            cqg[u, :, span, :] = jnp.where(p < size, rows[0:2], jnp.zeros_like(rows[0:2]))
+            ckv[u, :, span, :] = rows[2:4]
+        for array in range(2):
+            at = pl.ds(array * HD + head, 1)
+            lines = [hb[2 * u + slot, at, :] for slot in range(2)] + [jnp.zeros((14, DH), F32)]
+            ckv[u, array, ROWS:KEYS, :] = jnp.concatenate(lines, axis=0).astype(BF16)
+        for lo, hi in CHUNKS:
+            q = cqg[u, 0, lo:hi, :]
+            g = cqg[u, 1, lo:hi, :]
+            keys = ckv[u, 0]
+            values = ckv[u, 1]
+            mask = bias[u]
+            mask = jnp.concatenate([mask] * ((hi - lo) // BLK), axis=1)
+            score = nt(keys, q) * FACTOR + mask
+            top = jnp.max(score, axis=0, keepdims=True)
+            grown = jnp.exp(score - top)
+            prob = grown * (1.0 / jnp.sum(grown, axis=0, keepdims=True))
+            low = prob.astype(BF16)
+            dprob = nt(values, g)
+            delta = jnp.sum(low.astype(F32) * dprob, axis=0, keepdims=True)
+            mixing = (FACTOR * prob * (dprob - delta)).astype(BF16)
+            probs[u, :, lo:hi] = low
+            mixes[u, :, lo:hi] = mixing
+            q_grad = lax.dot_general(mixing, keys, (((0,), (0,)), ((), ())), preferred_element_type=F32)
+            gr[u, turn, 0, lo // BLK : hi // BLK] = q_grad.astype(BF16).reshape(-1, BLK, DH)
+        here = jnp.where(first, home_x(head).astype(jnp.int32), home_y(head).astype(jnp.int32)) > 0
+        for array, weights in ((0, mixes), (1, probs)):
+            total = jnp.dot(weights[u], cqg[u, array], preferred_element_type=F32)
+            gr[u, turn, 1 + array] = total[0:ROWS].astype(BF16).reshape(MOST, BLK, DH)
+            for slot in range(2):
+                line = total[ROWS + slot : ROWS + slot + 1]
+                hd[2 * u + slot, pl.ds(array * HD + head, 1), :] = jnp.where(here, line, 0.0)
+
+        for after, slots in enumerate(((0,), (1, 3), (2, 4, 5))):
+            for d in range(2):
+
+                @pl.when(n == after + 3 * d)
+                def _(d=d, slots=slots):
+                    for slot in slots:
                         if slot < CAP[d]:
                             send_back(d, slot)
 
         return carry
 
-    lax.fori_loop(0, HD, work, 0)
+    lax.fori_loop(0, 2 * HD, work, 0)
 
     tags = [jnp.full((1, DH), name).astype(F32) for name in names] + [jnp.full((12, DH), -1.0, F32)]
     block = jnp.concatenate([hd[slot] for slot in range(4)] + tags, axis=0)
@@ -378,7 +398,7 @@
             unit = jnp.where(in_x, unit_x, 1 - unit_x)
             when = jnp.where(in_x, HD - 1 - head, head)
             p = jnp.clip(jnp.where(in_x, j - start_x, j - start_y), 0, MOST - 1)
-            slot = jnp.where(in_x, head * b_x + j, (HD - 1 - head) * a_y + j - start_y)
+            slot = jnp.where(in_x, head * b_x + j, (HD - 1 - head) * a_y + 3 - j)
             here = jnp.where(in_x, home_x(head).astype(jnp.int32), home_y(head).astype(jnp.int32)) > 0
             most = jnp.where(unit == 1, CAP[0] - 1, CAP[1] - 1)
             at = 6 * (1 - unit) + jnp.clip(slot, 0, most)
@@ -443,8 +463,11 @@
             peer_copy(array, head).wait_send()
     for d in range(2):
         for slot in range(CAP[d]):
-            forward(d, slot).wait_send()
+            if d + slot > 0:
+                forward(d, slot).wait_send()
             give_back(d, slot).wait_send()
+    for array in range(4):
+        edge_copy(array).wait_send()
     for head in range(HD):
         for d in range(1, 4):
             deliver(d, head).wait_send()
@@ -520,6 +543,8 @@
             dma((HD, 3)),
             dma((HD, 3)),
             dma((HD,)),
+            dma((4,)),
+            dma((4,)),
             dma((5,)),
             dma((6,)),
             dma,

time: 106 us -> 105 us (level)
  the two profiles are of different devices: /device:TPU:7 before, /device:TPU:25 now
where the time goes in v4:
time: 105 us
  Pallas kernels  104 us (99%)
    pallas_call x1, Pallas kernels, body(): pl.pallas_call(kernel, out_shape=(grad, grad, grad, jax.ShapeDtypeStruct(...  101 us
    pallas_call x1, Pallas kernels, body(): pl.pallas_call(finish, out_shape=(grad, grad, grad, line, line), compiler...  2.54 us

profile of v4, /device:TPU:25, one launch (start us, length us, event | category | flops | bytes accessed | tf_op | source)
XLA Modules:
  0.0 104.6 jit_solution(9837336281183038627)
XLA Ops:
  0.6 101.5 %shard_map.146 = (bf16[128,2048]{1,0:T(8,128)(2,1)}, bf16[128,2048]{1,0:T(8,128)(2,1)}, bf16[128,2048]{1,0:T(8,128)(2,1)}, bf16[16,128]{1,0:T(8,128)(2,1)}) custom-call(bf16[2,128,1024]{2,1,0:T(8,128)(2,1)} %bitcast.6, bf16[2,128,1024]{2,1,0:T(8,128)(2,1)} %bitcast.7, bf16[2,128,1024]{2,1,0:T(8,128)(2,1)} %bitcast.8, bf16[2,128,1024]{2,1,0:T(8,128)(2,1)} %bitcast.9, ...), custom_call_target="tpu_custom_call" | custom-call | tf_op jit(solution)/shard_map/pallas_call | solution.py:504
  102.1 2.5 %shard_map.147 = (bf16[128,2048]{1,0:T(8,128)(2,1)}, bf16[128,2048]{1,0:T(8,128)(2,1)}, bf16[128,2048]{1,0:T(8,128)(2,1)}, bf16[1,1024]{1,0:T(2,128)(2,1)}, bf16[1,1024]{1,0:T(2,128)(2,1)}) custom-call(bf16[128,2048]{1,0:T(8,128)(2,1)} %get-tuple-element.9.q_in, bf16[128,2048]{1,0:T(8,128)(2,1)} %get-tuple-element.10.k_in, ...), custom_call_target="tpu_custom_call" | custom-call | tf_op jit(solution)/shard_map/pallas_call | solution.py:562

commit v5 on v4

--- a/solution.py
+++ b/solution.py
@@ -352,24 +352,7 @@
 
         return carry
 
-    lax.fori_loop(0, 2 * HD, work, 0)
-
-    tags = [jnp.full((1, DH), name).astype(F32) for name in names] + [jnp.full((12, DH), -1.0, F32)]
-    block = jnp.concatenate([hd[slot] for slot in range(4)] + tags, axis=0)
-    hz[pl.ds(z8, 1)] = block.astype(BF16)[None]
-
-    def out_z(d):
-        return remote(hz.at[z8], hz.at[z8], ht_send.at[d - 1], ht_recv.at[d - 1], z_peer(d), h)
-
-    def out_x(d):
-        return remote(hx.at[x4], hx.at[x4], ht_send.at[6 + d], ht_recv.at[6 + d], x_peer(d), h)
-
-    def out_y(d):
-        src = hs.at[lax.rem(j8 + d, 8)]
-        return remote(src, ry.at[j8], ht_send.at[9 + d], ht_recv.at[9 + d], y_peer(d), h)
-
-    for d in range(1, 8):
-        out_z(d).start()
+    lax.fori_loop(0, 2 * HD - 1, work, 0)
 
     mine = 2 * core + h
 
@@ -386,8 +369,8 @@
     def keep(head):
         return pltpu.make_async_copy(ost.at[head, mine], back.at[:, :, column(head)], xown_sem.at[head])
 
-    for slot in range(4):
-        for d in range(2):
+    for d in range(2):
+        for slot in range(CAP[d]):
             give_back(d, slot).wait_recv()
             rw[6 * d + slot] = rland[6 * d + slot]
     unit_x = jnp.where(core == 1, 0, 1)
@@ -412,11 +395,26 @@
     def assemble_pair(one, two):
         lax.fori_loop(0, 2, lambda i, carry: assemble(one + (two - one) * i, carry), 0)
 
+    assemble_pair(1, 2)
+    work(2 * HD - 1, 0)
+
+    tags = [jnp.full((1, DH), name).astype(F32) for name in names] + [jnp.full((12, DH), -1.0, F32)]
+    block = jnp.concatenate([hd[slot] for slot in range(4)] + tags, axis=0)
+    hz[pl.ds(z8, 1)] = block.astype(BF16)[None]
+
+    def out_z(d):
+        return remote(hz.at[z8], hz.at[z8], ht_send.at[d - 1], ht_recv.at[d - 1], z_peer(d), h)
+
+    def out_x(d):
+        return remote(hx.at[x4], hx.at[x4], ht_send.at[6 + d], ht_recv.at[6 + d], x_peer(d), h)
+
+    def out_y(d):
+        src = hs.at[lax.rem(j8 + d, 8)]
+        return remote(src, ry.at[j8], ht_send.at[9 + d], ht_recv.at[9 + d], y_peer(d), h)
+
+    for d in range(1, 8):
+        out_z(d).start()
     assemble_pair(0, 3)
-    for slot in range(4, 6):
-        give_back(0, slot).wait_recv()
-        rw[slot] = rland[slot]
-    assemble_pair(1, 2)
 
     for d in range(1, 8):
         out_z(d).wait_recv()

time: 105 us -> 107 us (1.019)
  the two profiles are of different devices: /device:TPU:25 before, /device:TPU:7 now
where the time goes in v5:
time: 107 us; the launch traced here: 105 us
  Pallas kernels  105 us (98%)
    pallas_call x1, Pallas kernels, body(): pl.pallas_call(kernel, out_shape=(grad, grad, grad, jax.ShapeDtypeStruct(...  102 us
    pallas_call x1, Pallas kernels, body(): pl.pallas_call(finish, out_shape=(grad, grad, grad, line, line), compiler...  2.54 us

profile of v5, /device:TPU:7, one launch (start us, length us, event | category | flops | bytes accessed | tf_op | source)
XLA Modules:
  0.0 105.3 jit_solution(240215756701018191)
XLA Ops:
  0.6 102.1 %shard_map.146 = (bf16[128,2048]{1,0:T(8,128)(2,1)}, bf16[128,2048]{1,0:T(8,128)(2,1)}, bf16[128,2048]{1,0:T(8,128)(2,1)}, bf16[16,128]{1,0:T(8,128)(2,1)}) custom-call(bf16[2,128,1024]{2,1,0:T(8,128)(2,1)} %bitcast.6, bf16[2,128,1024]{2,1,0:T(8,128)(2,1)} %bitcast.7, bf16[2,128,1024]{2,1,0:T(8,128)(2,1)} %bitcast.8, bf16[2,128,1024]{2,1,0:T(8,128)(2,1)} %bitcast.9, ...), custom_call_target="tpu_custom_call" | custom-call | tf_op jit(solution)/shard_map/pallas_call | solution.py:502
  102.8 2.5 %shard_map.147 = (bf16[128,2048]{1,0:T(8,128)(2,1)}, bf16[128,2048]{1,0:T(8,128)(2,1)}, bf16[128,2048]{1,0:T(8,128)(2,1)}, bf16[1,1024]{1,0:T(2,128)(2,1)}, bf16[1,1024]{1,0:T(2,128)(2,1)}) custom-call(bf16[128,2048]{1,0:T(8,128)(2,1)} %get-tuple-element.9.q_in, bf16[128,2048]{1,0:T(8,128)(2,1)} %get-tuple-element.10.k_in, ...), custom_call_target="tpu_custom_call" | custom-call | tf_op jit(solution)/shard_map/pallas_call | solution.py:560

commit v6 on v3

--- a/solution.py
+++ b/solution.py
@@ -19,7 +19,7 @@
 KEYS = ROWS + 16
 SEQ = 256
 CAP = (6, 4)
-CHUNKS = ((0, 256), (256, 512), (512, 640))
+CHUNKS = ((0, 384), (384, 640))
 
 
 def kernel(
@@ -299,8 +299,7 @@
                 keys = ckv[u, 0]
                 values = ckv[u, 1]
                 mask = bias[u]
-                if hi - lo == 256:
-                    mask = jnp.concatenate([mask, mask], axis=1)
+                mask = jnp.concatenate([mask] * ((hi - lo) // BLK), axis=1)
                 score = nt(keys, q) * FACTOR + mask
                 top = jnp.max(score, axis=0, keepdims=True)
                 grown = jnp.exp(score - top)

time: 106 us -> 105 us (level)
  no operation moved by 1% of the time
where the time goes in v6:
time: 105 us
  Pallas kernels  104 us (99%)
    pallas_call x1, Pallas kernels, body(): pl.pallas_call(kernel, out_shape=(grad, grad, grad, jax.ShapeDtypeStruct(...  102 us
    pallas_call x1, Pallas kernels, body(): pl.pallas_call(finish, out_shape=(grad, grad, grad, line, line), compiler...  2.54 us

profile of v6, /device:TPU:7, one launch (start us, length us, event | category | flops | bytes accessed | tf_op | source)
XLA Modules:
  0.0 105.0 jit_solution(11403425993063989378)
XLA Ops:
  0.6 101.9 %shard_map.146 = (bf16[128,2048]{1,0:T(8,128)(2,1)}, bf16[128,2048]{1,0:T(8,128)(2,1)}, bf16[128,2048]{1,0:T(8,128)(2,1)}, bf16[16,128]{1,0:T(8,128)(2,1)}) custom-call(bf16[2,128,1024]{2,1,0:T(8,128)(2,1)} %bitcast.6, bf16[2,128,1024]{2,1,0:T(8,128)(2,1)} %bitcast.7, bf16[2,128,1024]{2,1,0:T(8,128)(2,1)} %bitcast.8, bf16[2,128,1024]{2,1,0:T(8,128)(2,1)} %bitcast.9, ...), custom_call_target="tpu_custom_call" | custom-call | tf_op jit(solution)/shard_map/pallas_call | solution.py:480
  102.5 2.5 %shard_map.147 = (bf16[128,2048]{1,0:T(8,128)(2,1)}, bf16[128,2048]{1,0:T(8,128)(2,1)}, bf16[128,2048]{1,0:T(8,128)(2,1)}, bf16[1,1024]{1,0:T(2,128)(2,1)}, bf16[1,1024]{1,0:T(2,128)(2,1)}) custom-call(bf16[128,2048]{1,0:T(8,128)(2,1)} %get-tuple-element.9.q_in, bf16[128,2048]{1,0:T(8,128)(2,1)} %get-tuple-element.10.k_in, ...), custom_call_target="tpu_custom_call" | custom-call | tf_op jit(solution)/shard_map/pallas_call | solution.py:536
